TPU v7x, 32 devices: a whole 2x2x4 slice. The times are simulated.
32 devices in a mesh: tiles: 16 (over z, y, core), band: 2 (over x).
Axes of the slice: x: 2, y: 2, z: 4, core: 2. Of those that a mesh axis runs over, the one named last changes fastest.
Arguments:
- optical_depth: bfloat16 [256, 90, 4, 256], P('tiles', None, None, 'band'), may hold values from 0.00049972534 to 0.029907227
- albedo: bfloat16 [256, 90, 256], P('tiles', None, 'band'), may hold values from 0.69921875 to 0.96875
- insolation: bfloat16 [256, 256], P('tiles', 'band'), may hold values from 20 to 100
- sunlit: int32 [256, 2], P('tiles', 'band'), may hold values from 0 to 1, as said below
- point_weight: float32 [4], replicated, may hold values from 0.1 to 1
- anomaly: float32 [256, 90, 256], P('tiles', None, 'band'), may hold values from -6 to 6
Outputs:
- heating: float32 [256, 90, 256], P('tiles', None, 'band')
- smoothed: float32 [256, 90, 256], P('tiles', None, 'band')
Inputs may be any that keep to these rules, and one draw needn't show every extreme that they name: In every row, of two blocks that lie half of 2 sectors apart, exactly one is sunlit.
All inputs are finite; a program needn't handle non-finite values.
Results may differ from a plain program's by a relative error of at most 0.00045.
Values may be sent and summed in bfloat16 or wider, within the bound.
A program may use at most 64 MiB of HBM per device.

v0:
```python
import jax
import jax.numpy as jnp
from jax import lax
from jax.sharding import PartitionSpec as P

DIFF_STEPS = 4


slant_cosine = 0.5
mixing_rate = 0.2
base_loss = 0.005


def extended(x, sides, width):
    for axis, dim in sides:
        size, length = (lax.axis_size(axis), x.shape[dim])
        up = [(i, (i + 1) % size) for i in range(size)]
        down = [(j, i) for i, j in up]
        last = lax.slice_in_dim(x, length - width, length, axis=dim)
        first = lax.slice_in_dim(x, 0, width, axis=dim)
        before = lax.ppermute(last, axis, up)
        after = lax.ppermute(first, axis, down)
        x = jnp.concatenate([before, x, after], axis=dim)
    return x


def radiate(optical_depth, albedo, sunshine, point_weight):
    levels = optical_depth.shape[1]
    depth_all = optical_depth.astype(jnp.float32)
    albedo_all = albedo.astype(jnp.float32)
    sun_float = sunshine.astype(jnp.float32)[:, None, :]
    weights = point_weight[None, :, None]
    depth_now = jnp.zeros((depth_all.shape[0], depth_all.shape[2], depth_all.shape[3]), jnp.float32)
    link_prev = jnp.zeros((depth_all.shape[0], 1, depth_all.shape[3]), jnp.float32)
    ratio_prev = depth_now
    swept_prev = depth_now
    ratio_list = []
    swept_list = []
    extinct_list = []
    for level in range(levels):
        depth_layer = depth_all[:, level]
        albedo_now = albedo_all[:, level]
        if level + 1 < levels:
            albedo_next = albedo_all[:, level + 1]
        else:
            albedo_next = jnp.zeros_like(albedo_now)
        depth_new = depth_now + depth_layer
        extinct = sun_float * (
            jnp.exp(-depth_now / slant_cosine) - jnp.exp(-depth_new / slant_cosine)
        )
        link_next = (albedo_now * albedo_next)[:, None, :]
        diagonal = (
            base_loss + 2.0 * (1.0 - albedo_now)[:, None, :] * depth_layer + link_prev + link_next
        )
        pivot = diagonal - link_prev * ratio_prev
        ratio_now = link_next / pivot
        swept_now = (albedo_now[:, None, :] * extinct + link_prev * swept_prev) / pivot
        ratio_list.append(ratio_now)
        swept_list.append(swept_now)
        extinct_list.append(extinct)
        depth_now = depth_new
        link_prev = link_next
        ratio_prev = ratio_now
        swept_prev = swept_now
    flux_next = jnp.zeros_like(depth_now)
    heat_list = [None] * levels
    for level in range(levels - 1, -1, -1):
        diffuse_flux = swept_list[level] + ratio_list[level] * flux_next
        flux_next = diffuse_flux
        absorbed = (1.0 - albedo_all[:, level])[:, None, :] * (
            extinct_list[level] + 2.0 * depth_all[:, level] * diffuse_flux
        )
        heat_list[level] = jnp.sum(absorbed * weights, axis=1)
    return jnp.stack(heat_list, axis=1)


def per_device(optical_depth, albedo, insolation, sunlit, point_weight, anomaly):
    daylit = sunlit[:, 0]
    sunshine = jnp.where(daylit[:, None] == 1, insolation, jnp.zeros_like(insolation))
    heating = radiate(optical_depth, albedo, sunshine, point_weight)
    field_now = anomaly + heating
    at_top = lax.axis_index("tiles") == 0
    at_bottom = lax.axis_index("tiles") == lax.axis_size("tiles") - 1
    for sweep in range(DIFF_STEPS):
        padded = extended(field_now, (("tiles", 0), ("band", 2)), 1)
        row_above = jnp.where(at_top, 0.0, padded[0:1, :, 1:-1])
        row_below = jnp.where(at_bottom, 0.0, padded[-1:, :, 1:-1])
        centre = padded[1:-1, :, 1:-1]
        north_south = jnp.concatenate([centre[1:], row_below], axis=0) + jnp.concatenate(
            [row_above, centre[:-1]], axis=0
        )
        east_west = padded[1:-1, :, :-2] + padded[1:-1, :, 2:]
        field_now = field_now + mixing_rate * (north_south + east_west - 4.0 * field_now)
    return (heating, field_now)


def solution(mesh):
    placed = (
        P("tiles", None, None, "band"),
        P("tiles", None, "band"),
        P("tiles", "band"),
        P("tiles", "band"),
        P(),
        P("tiles", None, "band"),
    )
    return jax.shard_map(
        per_device,
        mesh=mesh,
        in_specs=placed,
        out_specs=(P("tiles", None, "band"), P("tiles", None, "band")),
        check_vma=False,
    )
```

profile of v0, /device:TPU:0, one launch (start us, length us, event | category | flops | bytes accessed | tf_op | source)
XLA Modules:
  0.0 90.0 jit_solution(16675599096269893620)
XLA Ops:
  0.6 1.0 %convert_element_type.9 = f32[16,90,128]{2,0,1:T(8,128)S(1)} convert(bf16[16,90,128]{2,0,1:T(8,128)(2,1)} %param.7) | non-fusion elementwise | flops 184320 | bytes 1105920 | tf_op jit(solution)/shard_map/convert_element_type | solution.py:30
  2.6 0.7 copy-done.1
  4.2 4.1 %add_divide_fusion.42 = (f32[16,4,128]{2,0,1:T(8,128)S(1)}, f32[16,4,128]{2,0,1:T(8,128)S(1)}, f32[16,4,128]{2,0,1:T(8,128)S(1)}, f32[16,4,128]{2,0,1:T(8,128)S(...) fusion(f32[16,128]{1,0:T(8,128)S(1)} %get-tuple-element.616, ...), kind=kLoop, calls=%fused_computation.590 | loop fusion | flops 5521408 | bytes 6651904 | tf_op jit(solution)/shard_map/div | solution.py:57
  8.4 4.1 %add_divide_fusion = (f32[16,4,128]{2,0,1:T(8,128)S(1)}, f32[16,4,128]{2,0,1:T(8,128)S(1)}, f32[16,4,128]{2,0,1:T(8,128)S(1)}, f32[16,4,128]{2,0,1:T(8,128)S(1)}...) fusion(f32[16,128]{1,0:T(8,128)S(1)} %get-tuple-element.725, ...), kind=kLoop, calls=%fused_computation.422 | loop fusion | flops 5521408 | bytes 6651904 | tf_op jit(solution)/shard_map/div | solution.py:57
  12.7 0.5 copy-done.4
  16.8 0.8 copy-done.2
  17.7 0.5 collective-permute-start.1
  18.2 5.1 %collective-permute-start = (f32[1,90,128]{2,0,1:T(1,128)S(1)}, f32[1,90,128]{2,0,1:T(1,128)S(1)}, u32[]{:S(2)}, u32[]{:S(2)}) collective-permute-start(f32[1,90,128]{2,0,1:T(1,128)S(1)} %get-tuple-element.462), channel_id=1, source_target_pairs={{2,0},{4,2},{6,4},{8,6},{10,8},{12,10},{14,12},{16,14},{18,16},{20... | collective-permute-start | bytes 138248 | tf_op jit(solution)/shard_map/ppermute | solution.py:22
  23.2 1.0 %fusion.164 = (f32[15,90,128]{2,0,1:T(8,128)S(1)}, f32[15,90,128]{2,0,1:T(8,128)}) fusion(f32[16,90,128]{2,0,1:T(8,128)S(1)} %add.3636), kind=kLoop, calls=%fused_computation.1326 | loop fusion | bytes 2764800 | tf_op jit(solution)/shard_map/slice | solution.py:90
  24.2 0.8 collective-permute-done.1
  25.2 1.3 %fusion.157 = (f32[18,90,1]{2,0,1:T(8,128)}, f32[18,90,1]{2,0,1:T(8,128)S(1)}) fusion(f32[18,90,128]{2,0,1:T(8,128)S(1)} %pad_maximum_fusion), kind=kLoop, calls=%fused_computation.1319 | loop fusion | bytes 25920 | tf_op jit(solution)/shard_map/slice | solution.py:19
  26.5 1.6 %copy.295 = f32[18,90,1]{1,0,2:T(8,128)S(1)} copy(f32[18,90,1]{2,0,1:T(8,128)} %get-tuple-element.445) | data formatting | bytes 12960 | tf_op jit(solution)/shard_map/slice | solution.py:19
  28.1 0.4 copy.297
  28.6 1.9 %collective-permute-start.3 = (f32[18,90,1]{1,0,2:T(8,128)S(1)}, f32[18,90,1]{1,0,2:T(8,128)S(1)}, u32[]{:S(2)}, u32[]{:S(2)}) collective-permute-start(f32[18,90,1]{1,0,2:T(8,128)S(1)} %copy.297), channel_id=1, source_target_pairs={{1,0},{0,1},{3,2},{2,3},{5,4},{4,5},{7,6},{6,7},{9,8},{8,9},{11,10... | collective-permute-start | bytes 19448 | tf_op jit(solution)/shard_map/ppermute | solution.py:22
  30.7 3.5 %collective-permute-done.2 = f32[18,90,1]{1,0,2:T(8,128)S(1)} collective-permute-done((f32[18,90,1]{1,0,2:T(8,128)S(1)}, f32[18,90,1]{1,0,2:T(8,128)S(1)}, u32[]{:S(2)}, u32[]{:S(2)}) %collective-permute-start.2) | collective-permute-done | bytes 6512 | tf_op jit(solution)/shard_map/ppermute | solution.py:21
  34.2 0.5 copy.296
  34.7 1.4 %copy.298 = f32[18,90,1]{2,0,1:T(8,128)} copy(f32[18,90,1]{1,0,2:T(8,128)S(1)} %collective-permute-done.3) | data formatting | bytes 12960 | tf_op jit(solution)/shard_map/ppermute | solution.py:22
  36.1 2.4 %fusion.19 = f32[16,90,128]{2,0,1:T(8,128)S(1)} fusion(f32[16,90,128]{2,0,1:T(8,128)S(1)} %add.3636, f32[18,90,1]{2,0,1:T(8,128)} %copy.298, f32[1,90,128]{2,0,1:T(1,128)S(1)} %collective-permute-done, f32[1,90,128]{2,0,1:T(1,128)S(1)} %collective-permute-done.1, f32[18,90,1]{2,0,1:T(8,128)S(1)} %copy.296, f32[1,90,128]{2,0,1:T(1,128)S(1)} %broadcast_select_fusion.7, ...), kind=kLoop, calls=%fused_computation.43 | loop fusion | flops 2764800 | bytes 3054240 | tf_op jit(solution)/shard_map/add | solution.py:93
  38.7 4.4 %collective-permute-start.4 = (f32[1,90,128]{2,0,1:T(1,128)S(1)}, f32[1,90,128]{2,0,1:T(1,128)S(1)}, u32[]{:S(2)}, u32[]{:S(2)}) collective-permute-start(f32[1,90,128]{2,0,1:T(1,128)S(1)} %get-tuple-element.458), channel_id=1, source_target_pairs={{2,0},{4,2},{6,4},{8,6},{10,8},{12,10},{14,12},{16,14},{18,16},{20... | collective-permute-start | bytes 138248 | tf_op jit(solution)/shard_map/ppermute | solution.py:22
  43.1 1.2 %fusion.162 = (f32[15,90,128]{2,0,1:T(8,128)}, f32[15,90,128]{2,0,1:T(8,128)}) fusion(f32[16,90,128]{2,0,1:T(8,128)S(1)} %fusion.19), kind=kLoop, calls=%fused_computation.1324 | loop fusion | bytes 2764800 | tf_op jit(solution)/shard_map/slice | solution.py:90
  44.4 0.5 collective-permute-done.5
  45.4 0.4 copy.299
  45.8 0.4 copy.301
  46.4 1.9 %collective-permute-start.6 = (f32[18,90,1]{1,0,2:T(8,128)S(1)}, f32[18,90,1]{1,0,2:T(8,128)S(1)}, u32[]{:S(2)}, u32[]{:S(2)}) collective-permute-start(f32[18,90,1]{1,0,2:T(8,128)S(1)} %copy.299), channel_id=1, source_target_pairs={{0,1},{1,0},{2,3},{3,2},{4,5},{5,4},{6,7},{7,6},{8,9},{9,8},{10,11... | collective-permute-start | bytes 19448 | tf_op jit(solution)/shard_map/ppermute | solution.py:21
  48.4 1.7 %collective-permute-done.6 = f32[18,90,1]{1,0,2:T(8,128)S(1)} collective-permute-done((f32[18,90,1]{1,0,2:T(8,128)S(1)}, f32[18,90,1]{1,0,2:T(8,128)S(1)}, u32[]{:S(2)}, u32[]{:S(2)}) %collective-permute-start.6) | collective-permute-done | bytes 6512 | tf_op jit(solution)/shard_map/ppermute | solution.py:21
  50.1 0.5 copy.300
  50.6 1.4 %copy.302 = f32[18,90,1]{2,0,1:T(8,128)} copy(f32[18,90,1]{1,0,2:T(8,128)S(1)} %collective-permute-done.7) | data formatting | bytes 12960 | tf_op jit(solution)/shard_map/ppermute | solution.py:22
  52.1 2.4 %fusion.14 = f32[16,90,128]{2,0,1:T(8,128)S(1)} fusion(f32[16,90,128]{2,0,1:T(8,128)S(1)} %fusion.19, f32[18,90,1]{2,0,1:T(8,128)} %copy.302, f32[1,90,128]{2,0,1:T(1,128)S(1)} %collective-permute-done.4, f32[1,90,128]{2,0,1:T(1,128)S(1)} %collective-permute-done.5, f32[18,90,1]{2,0,1:T(8,128)S(1)} %copy.300, f32[1,90,128]{2,0,1:T(1,128)S(1)} %broadcast_select_fusion.6, ...), kind=kLoop, calls=%fused_computation.32 | loop fusion | flops 2764800 | bytes 3054240 | tf_op jit(solution)/shard_map/add | solution.py:93
  54.6 4.4 %collective-permute-start.8 = (f32[1,90,128]{2,0,1:T(1,128)S(1)}, f32[1,90,128]{2,0,1:T(1,128)S(1)}, u32[]{:S(2)}, u32[]{:S(2)}) collective-permute-start(f32[1,90,128]{2,0,1:T(1,128)S(1)} %get-tuple-element.454), channel_id=1, source_target_pairs={{2,0},{4,2},{6,4},{8,6},{10,8},{12,10},{14,12},{16,14},{18,16},{20... | collective-permute-start | bytes 138248 | tf_op jit(solution)/shard_map/ppermute | solution.py:22
  59.0 1.0 %fusion.160 = (f32[15,90,128]{2,0,1:T(8,128)S(1)}, f32[15,90,128]{2,0,1:T(8,128)}) fusion(f32[16,90,128]{2,0,1:T(8,128)S(1)} %fusion.14), kind=kLoop, calls=%fused_computation.1322 | loop fusion | bytes 2764800 | tf_op jit(solution)/shard_map/slice | solution.py:90
  60.0 0.8 collective-permute-done.9
  61.0 1.3 %fusion.155 = (f32[18,90,1]{2,0,1:T(8,128)}, f32[18,90,1]{2,0,1:T(8,128)S(1)}) fusion(f32[18,90,128]{2,0,1:T(8,128)S(1)} %pad_maximum_fusion.2), kind=kLoop, calls=%fused_computation.1317 | loop fusion | bytes 25920 | tf_op jit(solution)/shard_map/slice | solution.py:19
  62.3 1.6 %copy.303 = f32[18,90,1]{1,0,2:T(8,128)S(1)} copy(f32[18,90,1]{2,0,1:T(8,128)} %get-tuple-element.441) | data formatting | bytes 12960 | tf_op jit(solution)/shard_map/slice | solution.py:19
  64.0 0.4 copy.305
  64.4 1.9 %collective-permute-start.11 = (f32[18,90,1]{1,0,2:T(8,128)S(1)}, f32[18,90,1]{1,0,2:T(8,128)S(1)}, u32[]{:S(2)}, u32[]{:S(2)}) collective-permute-start(f32[18,90,1]{1,0,2:T(8,128)S(1)} %copy.305), channel_id=1, source_target_pairs={{1,0},{0,1},{3,2},{2,3},{5,4},{4,5},{7,6},{6,7},{9,8},{8,9},{11,10... | collective-permute-start | bytes 19448 | tf_op jit(solution)/shard_map/ppermute | solution.py:22
  66.6 3.5 %collective-permute-done.10 = f32[18,90,1]{1,0,2:T(8,128)S(1)} collective-permute-done((f32[18,90,1]{1,0,2:T(8,128)S(1)}, f32[18,90,1]{1,0,2:T(8,128)S(1)}, u32[]{:S(2)}, u32[]{:S(2)}) %collective-permute-start.10) | collective-permute-done | bytes 6512 | tf_op jit(solution)/shard_map/ppermute | solution.py:21
  70.0 0.5 copy.304
  70.5 1.4 %copy.306 = f32[18,90,1]{2,0,1:T(8,128)} copy(f32[18,90,1]{1,0,2:T(8,128)S(1)} %collective-permute-done.11) | data formatting | bytes 12960 | tf_op jit(solution)/shard_map/ppermute | solution.py:22
  72.0 2.4 %fusion.9 = f32[16,90,128]{2,0,1:T(8,128)S(1)} fusion(f32[16,90,128]{2,0,1:T(8,128)S(1)} %fusion.14, f32[18,90,1]{2,0,1:T(8,128)} %copy.306, f32[1,90,128]{2,0,1:T(1,128)S(1)} %collective-permute-done.8, f32[1,90,128]{2,0,1:T(1,128)S(1)} %collective-permute-done.9, f32[18,90,1]{2,0,1:T(8,128)S(1)} %copy.304, f32[1,90,128]{2,0,1:T(1,128)S(1)} %broadcast_select_fusion.5, ...), kind=kLoop, calls=%fused_computation.21 | loop fusion | flops 2764800 | bytes 3054240 | tf_op jit(solution)/shard_map/add | solution.py:93
  74.5 4.4 %collective-permute-start.12 = (f32[1,90,128]{2,0,1:T(1,128)S(1)}, f32[1,90,128]{2,0,1:T(1,128)S(1)}, u32[]{:S(2)}, u32[]{:S(2)}) collective-permute-start(f32[1,90,128]{2,0,1:T(1,128)S(1)} %get-tuple-element.450), channel_id=1, source_target_pairs={{2,0},{4,2},{6,4},{8,6},{10,8},{12,10},{14,12},{16,14},{18,16},{20... | collective-permute-start | bytes 138248 | tf_op jit(solution)/shard_map/ppermute | solution.py:22
  78.9 1.2 %fusion.158 = (f32[15,90,128]{2,0,1:T(8,128)}, f32[15,90,128]{2,0,1:T(8,128)}) fusion(f32[16,90,128]{2,0,1:T(8,128)S(1)} %fusion.9), kind=kLoop, calls=%fused_computation.1320 | loop fusion | bytes 2764800 | tf_op jit(solution)/shard_map/slice | solution.py:90
  80.2 0.5 collective-permute-done.13
  81.6 0.4 copy.309
  82.2 1.9 %collective-permute-start.14 = (f32[18,90,1]{1,0,2:T(8,128)S(1)}, f32[18,90,1]{1,0,2:T(8,128)S(1)}, u32[]{:S(2)}, u32[]{:S(2)}) collective-permute-start(f32[18,90,1]{1,0,2:T(8,128)S(1)} %copy.307), channel_id=1, source_target_pairs={{0,1},{1,0},{2,3},{3,2},{4,5},{5,4},{6,7},{7,6},{8,9},{9,8},{10,11... | collective-permute-start | bytes 19448 | tf_op jit(solution)/shard_map/ppermute | solution.py:21
  84.2 1.7 %collective-permute-done.14 = f32[18,90,1]{1,0,2:T(8,128)S(1)} collective-permute-done((f32[18,90,1]{1,0,2:T(8,128)S(1)}, f32[18,90,1]{1,0,2:T(8,128)S(1)}, u32[]{:S(2)}, u32[]{:S(2)}) %collective-permute-start.14) | collective-permute-done | bytes 6512 | tf_op jit(solution)/shard_map/ppermute | solution.py:21
  85.9 0.5 copy.308
  86.4 0.5 copy.310
  86.9 3.1 %fusion.4 = f32[16,90,128]{2,0,1:T(8,128)} fusion(f32[16,90,128]{2,0,1:T(8,128)S(1)} %fusion.9, f32[18,90,1]{2,0,1:T(8,128)S(1)} %copy.310, f32[1,90,128]{2,0,1:T(1,128)S(1)} %collective-permute-done.12, f32[1,90,128]{2,0,1:T(1,128)S(1)} %collective-permute-done.13, f32[18,90,1]{2,0,1:T(8,128)S(1)} %copy.308, f32[1,90,128]{2,0,1:T(1,128)S(1)} %broadcast_select_fusion.4, ...), kind=kLoop, calls=%fused_computation.10 | loop fusion | flops 2764800 | bytes 3054240 | tf_op jit(solution)/shard_map/add | solution.py:93
  (200 shorter events, 7.9 us)
Async XLA Ops:
  2.0 0.7 copy-start.6
  2.0 1.4 %copy-start.1 = (bf16[16,90,4,128]{3,2,1,0:T(4,128)(2,1)S(1)}, bf16[16,90,4,128]{3,2,1,0:T(4,128)(2,1)}, u32[]{:S(2)}) copy-start(bf16[16,90,4,128]{3,2,1,0:T(4,128)(2,1)} %param.6) | copy-start | bytes 4423684
  3.4 0.7 copy-start.5
  12.5 0.7 copy-start.4
  15.6 1.1 %copy-start.3 = (f32[16,90,128]{2,0,1:T(8,128)S(1)}, f32[16,90,128]{2,0,1:T(8,128)}, u32[]{:S(2)}) copy-start(f32[16,90,128]{2,0,1:T(8,128)} %param.11) | copy-start | bytes 2211844
  16.7 0.9 copy-start.2
  17.7 7.3 %collective-permute-start.1 = (f32[1,90,128]{2,0,1:T(1,128)S(1)}, f32[1,90,128]{2,0,1:T(1,128)S(1)}, u32[]{:S(2)}, u32[]{:S(2)}) collective-permute-start(f32[1,90,128]{2,0,1:T(1,128)S(1)} %get-tuple-element.461), channel_id=1, source_target_pairs={{0,2},{2,4},{4,6},{6,8},{8,10},{10,12},{12,14},{14,16},{16,18},{18... | collective-permute-start | bytes 138248 | tf_op jit(solution)/shard_map/ppermute | solution.py:21
  18.2 6.8 %collective-permute-start = (f32[1,90,128]{2,0,1:T(1,128)S(1)}, f32[1,90,128]{2,0,1:T(1,128)S(1)}, u32[]{:S(2)}, u32[]{:S(2)}) collective-permute-start(f32[1,90,128]{2,0,1:T(1,128)S(1)} %get-tuple-element.462), channel_id=1, source_target_pairs={{2,0},{4,2},{6,4},{8,6},{10,8},{12,10},{14,12},{16,14},{18,16},{20... | collective-permute-start | bytes 138248 | tf_op jit(solution)/shard_map/ppermute | solution.py:22
  28.6 6.1 %collective-permute-start.3 = (f32[18,90,1]{1,0,2:T(8,128)S(1)}, f32[18,90,1]{1,0,2:T(8,128)S(1)}, u32[]{:S(2)}, u32[]{:S(2)}) collective-permute-start(f32[18,90,1]{1,0,2:T(8,128)S(1)} %copy.297), channel_id=1, source_target_pairs={{1,0},{0,1},{3,2},{2,3},{5,4},{4,5},{7,6},{6,7},{9,8},{8,9},{11,10... | collective-permute-start | bytes 19448 | tf_op jit(solution)/shard_map/ppermute | solution.py:22
  30.5 3.7 %collective-permute-start.2 = (f32[18,90,1]{1,0,2:T(8,128)S(1)}, f32[18,90,1]{1,0,2:T(8,128)S(1)}, u32[]{:S(2)}, u32[]{:S(2)}) collective-permute-start(f32[18,90,1]{1,0,2:T(8,128)S(1)} %copy.295), channel_id=1, source_target_pairs={{0,1},{1,0},{2,3},{3,2},{4,5},{5,4},{6,7},{7,6},{8,9},{9,8},{10,11... | collective-permute-start | bytes 19448 | tf_op jit(solution)/shard_map/ppermute | solution.py:21
  38.6 6.2 %collective-permute-start.5 = (f32[1,90,128]{2,0,1:T(1,128)S(1)}, f32[1,90,128]{2,0,1:T(1,128)S(1)}, u32[]{:S(2)}, u32[]{:S(2)}) collective-permute-start(f32[1,90,128]{2,0,1:T(1,128)S(1)} %get-tuple-element.457), channel_id=1, source_target_pairs={{0,2},{2,4},{4,6},{6,8},{8,10},{10,12},{12,14},{14,16},{16,18},{18... | collective-permute-start | bytes 138248 | tf_op jit(solution)/shard_map/ppermute | solution.py:21
  38.7 6.2 %collective-permute-start.4 = (f32[1,90,128]{2,0,1:T(1,128)S(1)}, f32[1,90,128]{2,0,1:T(1,128)S(1)}, u32[]{:S(2)}, u32[]{:S(2)}) collective-permute-start(f32[1,90,128]{2,0,1:T(1,128)S(1)} %get-tuple-element.458), channel_id=1, source_target_pairs={{2,0},{4,2},{6,4},{8,6},{10,8},{12,10},{14,12},{16,14},{18,16},{20... | collective-permute-start | bytes 138248 | tf_op jit(solution)/shard_map/ppermute | solution.py:22
  46.2 4.4 %collective-permute-start.7 = (f32[18,90,1]{1,0,2:T(8,128)S(1)}, f32[18,90,1]{1,0,2:T(8,128)S(1)}, u32[]{:S(2)}, u32[]{:S(2)}) collective-permute-start(f32[18,90,1]{1,0,2:T(8,128)S(1)} %copy.301), channel_id=1, source_target_pairs={{1,0},{0,1},{3,2},{2,3},{5,4},{4,5},{7,6},{6,7},{9,8},{8,9},{11,10... | collective-permute-start | bytes 19448 | tf_op jit(solution)/shard_map/ppermute | solution.py:22
  46.4 3.7 %collective-permute-start.6 = (f32[18,90,1]{1,0,2:T(8,128)S(1)}, f32[18,90,1]{1,0,2:T(8,128)S(1)}, u32[]{:S(2)}, u32[]{:S(2)}) collective-permute-start(f32[18,90,1]{1,0,2:T(8,128)S(1)} %copy.299), channel_id=1, source_target_pairs={{0,1},{1,0},{2,3},{3,2},{4,5},{5,4},{6,7},{7,6},{8,9},{9,8},{10,11... | collective-permute-start | bytes 19448 | tf_op jit(solution)/shard_map/ppermute | solution.py:21
  48.4 3.7 %copy-start = (f32[15,90,128]{2,0,1:T(8,128)S(1)}, f32[15,90,128]{2,0,1:T(8,128)}, u32[]{:S(2)}) copy-start(f32[15,90,128]{2,0,1:T(8,128)} %get-tuple-element.455) | copy-start | bytes 2073604
  54.6 6.2 %collective-permute-start.9 = (f32[1,90,128]{2,0,1:T(1,128)S(1)}, f32[1,90,128]{2,0,1:T(1,128)S(1)}, u32[]{:S(2)}, u32[]{:S(2)}) collective-permute-start(f32[1,90,128]{2,0,1:T(1,128)S(1)} %get-tuple-element.453), channel_id=1, source_target_pairs={{0,2},{2,4},{4,6},{6,8},{8,10},{10,12},{12,14},{14,16},{16,18},{18... | collective-permute-start | bytes 138248 | tf_op jit(solution)/shard_map/ppermute | solution.py:21
  54.6 6.2 %collective-permute-start.8 = (f32[1,90,128]{2,0,1:T(1,128)S(1)}, f32[1,90,128]{2,0,1:T(1,128)S(1)}, u32[]{:S(2)}, u32[]{:S(2)}) collective-permute-start(f32[1,90,128]{2,0,1:T(1,128)S(1)} %get-tuple-element.454), channel_id=1, source_target_pairs={{2,0},{4,2},{6,4},{8,6},{10,8},{12,10},{14,12},{16,14},{18,16},{20... | collective-permute-start | bytes 138248 | tf_op jit(solution)/shard_map/ppermute | solution.py:22
  64.4 6.1 %collective-permute-start.11 = (f32[18,90,1]{1,0,2:T(8,128)S(1)}, f32[18,90,1]{1,0,2:T(8,128)S(1)}, u32[]{:S(2)}, u32[]{:S(2)}) collective-permute-start(f32[18,90,1]{1,0,2:T(8,128)S(1)} %copy.305), channel_id=1, source_target_pairs={{1,0},{0,1},{3,2},{2,3},{5,4},{4,5},{7,6},{6,7},{9,8},{8,9},{11,10... | collective-permute-start | bytes 19448 | tf_op jit(solution)/shard_map/ppermute | solution.py:22
  66.3 3.7 %collective-permute-start.10 = (f32[18,90,1]{1,0,2:T(8,128)S(1)}, f32[18,90,1]{1,0,2:T(8,128)S(1)}, u32[]{:S(2)}, u32[]{:S(2)}) collective-permute-start(f32[18,90,1]{1,0,2:T(8,128)S(1)} %copy.303), channel_id=1, source_target_pairs={{0,1},{1,0},{2,3},{3,2},{4,5},{5,4},{6,7},{7,6},{8,9},{9,8},{10,11... | collective-permute-start | bytes 19448 | tf_op jit(solution)/shard_map/ppermute | solution.py:21
  74.4 6.2 %collective-permute-start.13 = (f32[1,90,128]{2,0,1:T(1,128)S(1)}, f32[1,90,128]{2,0,1:T(1,128)S(1)}, u32[]{:S(2)}, u32[]{:S(2)}) collective-permute-start(f32[1,90,128]{2,0,1:T(1,128)S(1)} %get-tuple-element.449), channel_id=1, source_target_pairs={{0,2},{2,4},{4,6},{6,8},{8,10},{10,12},{12,14},{14,16},{16,18},{18... | collective-permute-start | bytes 138248 | tf_op jit(solution)/shard_map/ppermute | solution.py:21
  74.5 6.2 %collective-permute-start.12 = (f32[1,90,128]{2,0,1:T(1,128)S(1)}, f32[1,90,128]{2,0,1:T(1,128)S(1)}, u32[]{:S(2)}, u32[]{:S(2)}) collective-permute-start(f32[1,90,128]{2,0,1:T(1,128)S(1)} %get-tuple-element.450), channel_id=1, source_target_pairs={{2,0},{4,2},{6,4},{8,6},{10,8},{12,10},{14,12},{16,14},{18,16},{20... | collective-permute-start | bytes 138248 | tf_op jit(solution)/shard_map/ppermute | solution.py:22
  82.1 4.4 %collective-permute-start.15 = (f32[18,90,1]{1,0,2:T(8,128)S(1)}, f32[18,90,1]{1,0,2:T(8,128)S(1)}, u32[]{:S(2)}, u32[]{:S(2)}) collective-permute-start(f32[18,90,1]{1,0,2:T(8,128)S(1)} %copy.309), channel_id=1, source_target_pairs={{1,0},{0,1},{3,2},{2,3},{5,4},{4,5},{7,6},{6,7},{9,8},{8,9},{11,10... | collective-permute-start | bytes 19448 | tf_op jit(solution)/shard_map/ppermute | solution.py:22
  82.2 3.7 %collective-permute-start.14 = (f32[18,90,1]{1,0,2:T(8,128)S(1)}, f32[18,90,1]{1,0,2:T(8,128)S(1)}, u32[]{:S(2)}, u32[]{:S(2)}) collective-permute-start(f32[18,90,1]{1,0,2:T(8,128)S(1)} %copy.307), channel_id=1, source_target_pairs={{0,1},{1,0},{2,3},{3,2},{4,5},{5,4},{6,7},{7,6},{8,9},{9,8},{10,11... | collective-permute-start | bytes 19448 | tf_op jit(solution)/shard_map/ppermute | solution.py:21
where the time goes:
time: 90.5 us; the launch traced here: 90 us
  starting transfers between devices  27.3 us (30%)
  other arithmetic  24.2 us (27%)
  local copies, waits for them, and re-layouts  23.7 us (26%)
  waiting for transfers between devices  12.9 us (14%)
  between operations  1.93 us (2%)
    ppermute x8, starting transfers between devices, extended(): after = lax.ppermute(first, axis, down)  22.6 us
    ppermute x8, waiting for transfers between devices, extended(): before = lax.ppermute(last, axis, up)  12.9 us
    add x4, other arithmetic, per_device(): field_now + mixing_rate * (north_south + east_west - 4.0 * field_now)  10.3 us
    div x3, other arithmetic, radiate(): (albedo_now[:, None, :] * extinct + link_prev * swept_prev) / pivot  8.36 us
    slice x12, local copies, waits for them, and re-layouts, extended(): last = lax.slice_in_dim(x, length - width, length, axis=dim)  7.75 us
    ppermute x4, local copies, waits for them, and re-layouts, extended(): after = lax.ppermute(first, axis, down)  4.84 us
    ppermute x8, starting transfers between devices, extended(): before = lax.ppermute(last, axis, up)  4.73 us
    slice x4, local copies, waits for them, and re-layouts, per_device(): centre[:-1]  4.4 us
  transfers between devices with their start and end apart: 16, of which 8 were waited for; matrix products, arithmetic and copies ran while one was open for 7% of the time, Pallas kernels for 0%

commit v1 on v0

v1 whole, which is shorter than its diff:
```python
import functools
import math

import jax
import jax.numpy as jnp
import numpy as np
from jax import lax
from jax.experimental import pallas as pl
from jax.experimental.pallas import tpu as pltpu
from jax.sharding import PartitionSpec as P

DIFF_STEPS = 4
HALO = 4
EDGE = 2 * HALO
UNROLL = 3

mixing_rate = 0.2
base_loss = 0.005

MESH = pl.DeviceIdType.MESH
F32 = jnp.float32


def edge_weights(rows):
    full = rows + 2 * HALO
    out = np.zeros((4, 2 * rows * EDGE, rows * EDGE), np.float64)
    columns = [np.ones(1)]
    for _ in range(DIFF_STEPS):
        columns.append(np.convolve(columns[-1], np.ones(3)))
    for variant in range(4):
        near = np.zeros((full, full))
        for i in range(full - 1):
            near[i, i + 1] = near[i + 1, i] = 1.0
        if variant & 1:
            near[:HALO] = 0.0
            near[:, :HALO] = 0.0
        if variant & 2:
            near[-HALO:] = 0.0
            near[:, -HALO:] = 0.0
        for k in range(DIFF_STEPS + 1):
            reach = DIFF_STEPS - k
            power = np.linalg.matrix_power(near, k) * math.comb(DIFF_STEPS, k)
            if k == 0 and variant & 1:
                power[:HALO, :HALO] = 0.0
            if k == 0 and variant & 2:
                power[-HALO:, -HALO:] = 0.0
            for q_to in range(EDGE):
                for q_from in range(EDGE):
                    if (q_to < HALO) == (q_from < HALO):
                        continue
                    gap = abs(q_to - q_from)
                    if gap > reach:
                        continue
                    weight = columns[reach][reach + gap] * mixing_rate**DIFF_STEPS
                    for r_to in range(rows):
                        for r_from in range(full):
                            if r_from < HALO:
                                lane = rows * EDGE + (rows - HALO + r_from) * EDGE
                            elif r_from < HALO + rows:
                                lane = (r_from - HALO) * EDGE
                            else:
                                lane = rows * EDGE + (r_from - HALO - rows) * EDGE
                            out[variant, lane + q_from, r_to * EDGE + q_to] += (
                                weight * power[HALO + r_to, r_from]
                            )
    return out.astype(np.float32)


def kernel(
    n_tiles, n_band, rows, levels, points,
    depth_hbm, albedo_hbm, anomaly_hbm, mats_hbm, insolation, sunlit, weight,
    heat_hbm, smooth_hbm,
    depth_in, albedo_in, anomaly_in, mats, sun, depth_f, albedo_f, swept, ratio, plain, heat_f,
    heat_out, field, smooth, strip, corner, got, got_corner,
    in_sem, out_sem, send_sem, recv_sem,
):
    lanes = field.shape[2]
    tile, band = lax.axis_index("tiles"), lax.axis_index("band")
    has_north, has_south = tile > 0, tile < n_tiles - 1
    north = lax.rem(tile + n_tiles - 1, n_tiles)
    south = lax.rem(tile + 1, n_tiles)
    sides = [lax.rem(band + 1, n_band)]
    if n_band > 2:
        sides.append(lax.rem(band + n_band - 1, n_band))
    n_sides = len(sides)
    per_tile = levels * points
    depth_step = per_tile + 1
    level_step = (levels + 7) // 8 * 8 + 1

    barrier = pltpu.get_barrier_semaphore()

    def greet(to_tile, to_band):
        pl.semaphore_signal(barrier, inc=1, device_id=(to_tile, to_band), device_id_type=MESH)

    for side in sides:
        greet(tile, side)

    @pl.when(has_north)
    def _():
        greet(north, band)
        for side in sides:
            greet(north, side)

    @pl.when(has_south)
    def _():
        greet(south, band)
        for side in sides:
            greet(south, side)

    groups = (((0, HALO), (rows - HALO, HALO)), ((HALO, rows - 2 * HALO),))
    loads = []
    for ranges in groups:
        mine = []
        for first, count in ranges:
            span = pl.ds(first * per_tile, count * per_tile)
            for source, target in (
                (depth_hbm.at[span], depth_in.at[span]),
                (albedo_hbm.at[pl.ds(first, count)], albedo_in.at[pl.ds(first, count)]),
            ):
                mine.append((source, target))
        loads.append(mine)
    copies, number = [], 0
    for mine in loads:
        started = []
        for source, target in mine:
            copy = pltpu.make_async_copy(source, target, in_sem.at[number])
            copy.start()
            started.append(copy)
            number += 1
        copies.append(started)
    anomaly_copy = pltpu.make_async_copy(anomaly_hbm, anomaly_in, in_sem.at[number])
    anomaly_copy.start()
    variant = jnp.where(has_north, 0, 1) + jnp.where(has_south, 0, 2)
    mats_copy = pltpu.make_async_copy(mats_hbm.at[variant], mats, in_sem.at[number + 1])
    mats_copy.start()

    lit = jnp.where(sunlit[...] == 1, insolation[...].astype(F32), 0.0)
    sun[pl.ds(0, HALO), :] = lit[:HALO]
    sun[pl.ds(HALO, HALO), :] = lit[rows - HALO :]
    sun[pl.ds(2 * HALO, rows - 2 * HALO), :] = lit[HALO : rows - HALO]
    weights = [weight[g] for g in range(points)]

    def row_of(slot, group):
        if group == 0:
            return slot if slot < HALO else rows - 2 * HALO + slot
        return HALO + slot

    def radiate(group):
        for copy in copies[group]:
            copy.wait()
        for slot in range(0, 8, 2):
            row = row_of(slot, group)
            pair = depth_in[pl.ds(row * per_tile, 2 * per_tile), :].astype(F32)
            depth_f[pl.ds(slot * depth_step, per_tile), :] = pair[:per_tile]
            depth_f[pl.ds((slot + 1) * depth_step, per_tile), :] = pair[per_tile:]
        for slot in range(8):
            albedo_f[pl.ds(slot * level_step, levels), :] = albedo_in[row_of(slot, group)].astype(F32)
            albedo_f[pl.ds(slot * level_step + levels, 1), :] = jnp.zeros((1, lanes), F32)

        def depth_at(level, g):
            return depth_f[pl.ds(level * points + g, 8, stride=depth_step), :]

        def albedo_at(level):
            return albedo_f[pl.ds(level, 8, stride=level_step), :]

        def down(step, carry):
            for inner in range(UNROLL):
                level = step * UNROLL + inner
                albedo_now, link_prev, state = carry
                albedo_next = albedo_at(level + 1)
                link = albedo_now * albedo_next
                base = base_loss + link_prev + link
                lost = 2.0 - 2.0 * albedo_now
                direct, later = None, []
                for g in range(points):
                    total, beam, p, m, s = state[g]
                    layer = depth_at(level, g)
                    total = total + layer
                    beam_new = jnp.exp(total * -2.0)
                    extinct = beam - beam_new
                    term = weights[g] * extinct
                    direct = term if direct is None else direct + term
                    p_new = (base + lost * layer) * p - link_prev * m
                    m_new = link * p
                    s_new = (albedo_now * extinct) * p + link_prev * s
                    guess = pl.reciprocal(p_new, approx=True)
                    inverse = guess * (2.0 - p_new * guess)
                    swept[level, g] = s_new * inverse
                    ratio[level, g] = m_new * inverse
                    later.append((total, beam_new, p_new, m_new, s_new))
                plain[level] = direct
                carry = (albedo_next, link, tuple(later))
            return carry

        zero = jnp.zeros((8, lanes), F32)
        one = jnp.ones((8, lanes), F32)
        start = (albedo_at(0), zero, tuple((zero, one, one, zero, zero) for _ in range(points)))
        lax.fori_loop(0, levels // UNROLL, down, start)

        sunshine = sun[pl.ds(8 * group, 8), :]

        def up(step, flux):
            for inner in range(UNROLL):
                level = levels - 1 - (step * UNROLL + inner)
                later, absorbed = [], None
                for g in range(points):
                    now = swept[level, g] + ratio[level, g] * flux[g]
                    term = (2.0 * weights[g]) * depth_at(level, g) * now
                    absorbed = term if absorbed is None else absorbed + term
                    later.append(now)
                flux = tuple(later)
                heat = (sunshine - sunshine * albedo_at(level)) * (plain[level] + absorbed)
                heat_f[pl.ds(level, 8, stride=level_step), :] = heat
            return flux

        lax.fori_loop(0, levels // UNROLL, up, tuple(zero for _ in range(points)))
        for slot in range(8):
            row = row_of(slot, group)
            heat = heat_f[pl.ds(slot * level_step, levels), :]
            heat_out[row] = heat
            field[HALO + row] = heat + anomaly_in[row]

    def by_levels(body):
        def step(j, _):
            body(pl.ds(pl.multiple_of(j * 8, 8), 8))
            return 0

        lax.fori_loop(0, levels // 8, step, 0)
        if levels % 8:
            body(pl.ds(levels - 8, 8))

    lane = lax.broadcasted_iota(jnp.int32, (8, lanes), 1)
    lane_row, lane_edge = lane // EDGE, lane % EDGE

    def gather_edges(start, wanted, span):
        value = start
        for place, index in wanted:
            moved = pltpu.roll(field[index, span, :], (place * EDGE + HALO) % lanes, 1)
            value = jnp.where(lane_row == place, moved, value)
        return value

    outer = [(r, HALO + r) for r in (*range(HALO), *range(rows - HALO, rows))]
    inner = [(r, HALO + r) for r in range(HALO, rows - HALO)]

    def remote(source, target, number, to_tile, to_band):
        return pltpu.make_async_remote_copy(
            src_ref=source, dst_ref=target, send_sem=send_sem.at[number], recv_sem=recv_sem.at[number],
            device_id=(to_tile, to_band), device_id_type=MESH,
        )

    to_north = [remote(field.at[pl.ds(HALO, HALO)], field.at[pl.ds(HALO + rows, HALO)], 0, north, band)]
    to_south = [remote(field.at[pl.ds(rows, HALO)], field.at[pl.ds(0, HALO)], 1, south, band)]
    to_side = []
    for j, side in enumerate(sides):
        to_north.append(remote(corner, got_corner.at[0, j], 2 + 3 * j, north, side))
        to_south.append(remote(corner, got_corner.at[1, j], 3 + 3 * j, south, side))
        to_side.append(remote(strip, got.at[j], 4 + 3 * j, tile, side))

    anomaly_copy.wait()
    radiate(0)

    def pack_outer(span):
        corner[span, :] = gather_edges(jnp.zeros((8, lanes), F32), outer, span)

    by_levels(pack_outer)

    peers = n_sides + (1 + n_sides) * (has_north.astype(jnp.int32) + has_south.astype(jnp.int32))
    pl.semaphore_wait(barrier, peers)

    @pl.when(has_north)
    def _():
        for copy in to_north:
            copy.start()

    @pl.when(has_south)
    def _():
        for copy in to_south:
            copy.start()

    @pl.when(jnp.logical_not(has_north))
    def _():
        field[pl.ds(0, HALO)] = jnp.zeros((HALO, levels, lanes), F32)
        for j in range(n_sides):
            got_corner[1, j] = jnp.zeros((levels, lanes), F32)

    @pl.when(jnp.logical_not(has_south))
    def _():
        field[pl.ds(HALO + rows, HALO)] = jnp.zeros((HALO, levels, lanes), F32)
        for j in range(n_sides):
            got_corner[0, j] = jnp.zeros((levels, lanes), F32)

    radiate(1)

    def pack_inner(span):
        strip[span, :] = gather_edges(corner[span, :], inner, span)

    by_levels(pack_inner)
    for copy in to_side:
        copy.start()
    heat_copy = pltpu.make_async_copy(heat_out, heat_hbm, out_sem.at[0])
    heat_copy.start()

    @pl.when(has_north)
    def _():
        for copy in to_south:
            copy.wait_recv()

    @pl.when(has_south)
    def _():
        for copy in to_north:
            copy.wait_recv()

    keep_north = jnp.where(has_north, 1.0, 0.0).astype(F32)
    keep_south = jnp.where(has_south, 1.0, 0.0).astype(F32)
    full = rows + 2 * HALO

    def diffuse(span):
        now = [field[i, span, :] for i in range(full)]
        for sweep in range(1, DIFF_STEPS + 1):
            later = [None] * full
            for i in range(sweep, full - sweep):
                x = now[i]
                value = (x + pltpu.roll(x, 1, 1)) + (pltpu.roll(x, lanes - 1, 1) + (now[i - 1] + now[i + 1]))
                if i < HALO:
                    value = value * keep_north
                if i >= HALO + rows:
                    value = value * keep_south
                later[i] = value
            now = later
        for r in range(rows):
            smooth[r, span, :] = now[HALO + r] * (mixing_rate**DIFF_STEPS)

    by_levels(diffuse)

    mats_copy.wait()
    for copy in to_side:
        copy.wait_recv()

    def pick(ref, span, *lead):
        west = ref[(*lead, 0, span, slice(None))]
        if n_sides == 1:
            return west
        return jnp.where(lane_edge < HALO, west, ref[(*lead, 1, span, slice(None))])

    beyond = [(rows - HALO + i, i) for i in range(HALO)] + [(i, HALO + rows + i) for i in range(HALO)]

    def differ(span):
        here = gather_edges(jnp.zeros((8, lanes), F32), beyond, span)
        there = jnp.where(
            lane_row < HALO,
            pick(got_corner, span, 0),
            jnp.where(lane_row >= rows - HALO, pick(got_corner, span, 1), 0.0),
        )
        return jnp.concatenate([pick(got, span) - strip[span, :], there - here], axis=1)

    def correct(span):
        fix = jnp.dot(
            differ(span), mats[...], precision=lax.Precision.HIGHEST, preferred_element_type=F32
        )
        for r in range(rows):
            moved = pltpu.roll(jnp.where(lane_row == r, fix, 0.0), (2 * lanes - r * EDGE - HALO) % lanes, 1)
            smooth[r, span, :] = smooth[r, span, :] + moved

    def correct_last(span):
        fix = jnp.dot(
            differ(span), mats[...], precision=lax.Precision.HIGHEST, preferred_element_type=F32
        )
        fresh = lax.broadcasted_iota(jnp.int32, (8, lanes), 0) >= 8 - levels % 8
        for r in range(rows):
            chosen = jnp.where((lane_row == r) & fresh, fix, 0.0)
            moved = pltpu.roll(chosen, (2 * lanes - r * EDGE - HALO) % lanes, 1)
            smooth[r, span, :] = smooth[r, span, :] + moved

    def correct_step(j, _):
        correct(pl.ds(pl.multiple_of(j * 8, 8), 8))
        return 0

    lax.fori_loop(0, levels // 8, correct_step, 0)
    if levels % 8:
        correct_last(pl.ds(levels - 8, 8))
    smooth_copy = pltpu.make_async_copy(smooth, smooth_hbm, out_sem.at[1])
    smooth_copy.start()

    @pl.when(has_north)
    def _():
        for copy in to_north:
            copy.wait_send()

    @pl.when(has_south)
    def _():
        for copy in to_south:
            copy.wait_send()

    for copy in to_side:
        copy.wait_send()
    heat_copy.wait()
    smooth_copy.wait()


def per_device(n_tiles, n_band, optical_depth, albedo, insolation, sunlit, point_weight, anomaly):
    rows, levels, points, lanes = optical_depth.shape
    n_sides = 1 if n_band == 2 else 2
    mats = edge_weights(rows)
    level_step = (levels + 7) // 8 * 8 + 1
    shape = jax.ShapeDtypeStruct((rows, levels, lanes), F32)
    vmem, smem, hbm = (pl.BlockSpec(memory_space=m) for m in (pltpu.VMEM, pltpu.SMEM, pl.ANY))
    n_copies = 2 + 3 * n_sides
    return pl.pallas_call(
        functools.partial(kernel, n_tiles, n_band, rows, levels, points),
        out_shape=(shape, shape),
        in_specs=[hbm, hbm, hbm, hbm, vmem, vmem, smem],
        out_specs=(hbm, hbm),
        scratch_shapes=[
            pltpu.VMEM((rows * levels * points, lanes), jnp.bfloat16),
            pltpu.VMEM((rows, levels, lanes), jnp.bfloat16),
            pltpu.VMEM((rows, levels, lanes), F32),
            pltpu.VMEM(mats.shape[1:], F32),
            pltpu.VMEM((rows, lanes), F32),
            pltpu.VMEM((8 * (levels * points + 1), lanes), F32),
            pltpu.VMEM((8 * level_step, lanes), F32),
            pltpu.VMEM((levels, points, 8, lanes), F32),
            pltpu.VMEM((levels, points, 8, lanes), F32),
            pltpu.VMEM((levels, 8, lanes), F32),
            pltpu.VMEM((8 * level_step, lanes), F32),
            pltpu.VMEM((rows, levels, lanes), F32),
            pltpu.VMEM((rows + 2 * HALO, levels, lanes), F32),
            pltpu.VMEM((rows, levels, lanes), F32),
            pltpu.VMEM((levels, lanes), F32),
            pltpu.VMEM((levels, lanes), F32),
            pltpu.VMEM((n_sides, levels, lanes), F32),
            pltpu.VMEM((2, n_sides, levels, lanes), F32),
            pltpu.SemaphoreType.DMA((8,)),
            pltpu.SemaphoreType.DMA((2,)),
            pltpu.SemaphoreType.DMA((n_copies,)),
            pltpu.SemaphoreType.DMA((n_copies,)),
        ],
        compiler_params=pltpu.CompilerParams(
            collective_id=0, has_side_effects=True, vmem_limit_bytes=40 * 1024 * 1024
        ),
    )(
        optical_depth.reshape(rows * levels * points, lanes), albedo, anomaly, jnp.asarray(mats),
        insolation, sunlit, point_weight,
    )


def solution(mesh):
    placed = (
        P("tiles", None, None, "band"),
        P("tiles", None, "band"),
        P("tiles", "band"),
        P("tiles", "band"),
        P(),
        P("tiles", None, "band"),
    )
    return jax.shard_map(
        functools.partial(per_device, mesh.shape["tiles"], mesh.shape["band"]),
        mesh=mesh,
        in_specs=placed,
        out_specs=(P("tiles", None, "band"), P("tiles", None, "band")),
        check_vma=False,
    )
```

time: 90.5 us -> 27.2 us (0.30)
  the two profiles are of different devices: /device:TPU:0 before, /device:TPU:9 now
where the time goes in v1:
time: 27.2 us; the launch traced here: 27 us
  Pallas kernels  20.4 us (75%)
  local copies, waits for them, and re-layouts  5.92 us (22%)
  between operations  0.71 us (3%)
    pallas_call x1, Pallas kernels, per_device(): pl.pallas_call(functools.partial(kernel, n_tiles, n_band, rows, levels, p...  20.4 us
    unnamed x11, local copies, waits for them, and re-layouts  3.33 us
    pallas_call x2, local copies, waits for them, and re-layouts, per_device(): pl.pallas_call(functools.partial(kernel, n_tiles, n_band, rows, levels, p...  2.59 us

profile of v1, /device:TPU:9, one launch (start us, length us, event | category | flops | bytes accessed | tf_op | source)
XLA Modules:
  0.0 27.0 jit_solution(1700055764183959189)
XLA Ops:
  0.6 0.0 copy-start.1
  0.6 0.0 copy-start.3
  0.7 0.0 copy-start.2
  0.7 0.0 copy-start
  0.7 0.9 %copy.11.sunlit = s32[16,1]{1,0:T(8,128)S(1)} copy(s32[16,1]{0,1:T(1,128)} %param.10) | data formatting | bytes 128 | tf_op args[3]
  1.5 1.1 %copy.9.albedo_hbm = bf16[16,90,128]{2,1,0:T(8,128)(2,1)S(1)} copy(bf16[16,90,128]{2,0,1:T(8,128)(2,1)} %param.8) | data formatting | bytes 737280 | tf_op args[1]
  2.6 1.4 %copy.10.anomaly_hbm = f32[16,90,128]{2,1,0:T(8,128)S(1)} copy(f32[16,90,128]{2,0,1:T(8,128)} %param.12) | data formatting | bytes 1474560 | tf_op args[5]
  4.0 0.0 copy-done.1
  4.0 0.0 copy-done.3
  4.0 0.0 copy-done.2
  4.0 0.0 copy-done
  4.0 20.4 %shard_map.86 = (f32[16,90,128]{2,1,0:T(8,128)S(1)}, f32[16,90,128]{2,1,0:T(8,128)S(1)}) custom-call(bf16[5760,128]{1,0:T(8,128)(2,1)S(1)} %bitcast.1, bf16[16,90,128]{2,1,0:T(8,128)(2,1)S(1)} %copy.9.albedo_hbm, f32[16,90,128]{2,1,0:T(8,128)S(1)} %copy.10.anomaly_hbm, f32[4,256,128]{2,1,0:T(8,128)S(1)} %copy-done.1, bf16[16,128]{1,0:T(8,128)(2,1)S(1)} %copy-done.2, ...), custom_call_target="tpu_custom_call" | custom-call | tf_op jit(solution)/shard_map/pallas_call | solution.py:408
  24.4 1.3 %copy.12 = f32[16,90,128]{2,0,1:T(8,128)} copy(f32[16,90,128]{2,1,0:T(8,128)S(1)} %get-tuple-element.2) | data formatting | bytes 1474560 | tf_op jit(solution)/shard_map/pallas_call | solution.py:408
  25.7 1.3 %copy.13 = f32[16,90,128]{2,0,1:T(8,128)} copy(f32[16,90,128]{2,1,0:T(8,128)S(1)} %get-tuple-element.3) | data formatting | bytes 1474560 | tf_op jit(solution)/shard_map/pallas_call | solution.py:408
Async XLA Ops:
  0.6 3.4 %copy-start.1 = (f32[4,256,128]{2,1,0:T(8,128)S(1)}, f32[4,256,128]{2,1,0:T(8,128)}, u32[]{:S(2)}) copy-start(f32[4,256,128]{2,1,0:T(8,128)} %constant.2.clone.mats_hbm) | copy-start | bytes 1572868
  0.6 3.4 %copy-start.3 = (f32[4]{0:T(128)S(1)}, f32[4]{0:T(128)}, u32[]{:S(2)}) copy-start(f32[4]{0:T(128)} %weight.1) | copy-start | bytes 52
  0.7 3.4 %copy-start.2 = (bf16[16,128]{1,0:T(8,128)(2,1)S(1)}, bf16[16,128]{1,0:T(8,128)(2,1)}, u32[]{:S(2)}) copy-start(bf16[16,128]{1,0:T(8,128)(2,1)} %insolation.1) | copy-start | bytes 12292
  0.7 3.4 %copy-start = (bf16[16,90,4,128]{3,2,1,0:T(4,128)(2,1)S(1)}, bf16[16,90,4,128]{3,2,1,0:T(4,128)(2,1)}, u32[]{:S(2)}) copy-start(bf16[16,90,4,128]{3,2,1,0:T(4,128)(2,1)} %param.7) | copy-start | bytes 4423684

commit v2 on v1

--- a/solution.py
+++ b/solution.py
@@ -12,7 +12,7 @@
 DIFF_STEPS = 4
 HALO = 4
 EDGE = 2 * HALO
-UNROLL = 3
+UNROLL = 9
 
 mixing_rate = 0.2
 base_loss = 0.005
@@ -70,11 +70,12 @@
     n_tiles, n_band, rows, levels, points,
     depth_hbm, albedo_hbm, anomaly_hbm, mats_hbm, insolation, sunlit, weight,
     heat_hbm, smooth_hbm,
-    depth_in, albedo_in, anomaly_in, mats, sun, depth_f, albedo_f, swept, ratio, plain, heat_f,
-    heat_out, field, smooth, strip, corner, got, got_corner,
+    depth_in, albedo_in, anomaly_in, mats, depth_f, swept, ratio, plain, heat_held,
+    heat_out, field, smooth, smooth_out, strip, corner, got, got_corner,
     in_sem, out_sem, send_sem, recv_sem,
 ):
-    lanes = field.shape[2]
+    lanes = field.shape[1]
+    half = rows // 2
     tile, band = lax.axis_index("tiles"), lax.axis_index("band")
     has_north, has_south = tile > 0, tile < n_tiles - 1
     north = lax.rem(tile + n_tiles - 1, n_tiles)
@@ -85,7 +86,8 @@
     n_sides = len(sides)
     per_tile = levels * points
     depth_step = per_tile + 1
-    level_step = (levels + 7) // 8 * 8 + 1
+    slab = (levels + 7) // 8 * 8 + 2
+    smooth_step = slab - 1
 
     barrier = pltpu.get_barrier_semaphore()
 
@@ -113,12 +115,9 @@
         mine = []
         for first, count in ranges:
             span = pl.ds(first * per_tile, count * per_tile)
-            for source, target in (
-                (depth_hbm.at[span], depth_in.at[span]),
-                (albedo_hbm.at[pl.ds(first, count)], albedo_in.at[pl.ds(first, count)]),
-            ):
-                mine.append((source, target))
+            mine.append((depth_hbm.at[span], depth_in.at[span]))
         loads.append(mine)
+    loads[0].append((albedo_hbm, albedo_in))
     copies, number = [], 0
     for mine in loads:
         started = []
@@ -134,16 +133,29 @@
     mats_copy = pltpu.make_async_copy(mats_hbm.at[variant], mats, in_sem.at[number + 1])
     mats_copy.start()
 
-    lit = jnp.where(sunlit[...] == 1, insolation[...].astype(F32), 0.0)
-    sun[pl.ds(0, HALO), :] = lit[:HALO]
-    sun[pl.ds(HALO, HALO), :] = lit[rows - HALO :]
-    sun[pl.ds(2 * HALO, rows - 2 * HALO), :] = lit[HALO : rows - HALO]
     weights = [weight[g] for g in range(points)]
+    sublane = lax.broadcasted_iota(jnp.int32, (half, lanes), 0)
+    front = sublane < HALO
 
     def row_of(slot, group):
         if group == 0:
-            return slot if slot < HALO else rows - 2 * HALO + slot
-        return HALO + slot
+            return slot if slot < HALO else half + slot
+        return half + slot if slot < HALO else slot
+
+    places = {row_of(slot, group): half * group + slot for group in range(2) for slot in range(half)}
+    for i in range(HALO):
+        places[i - HALO] = rows + i
+        places[rows + i] = rows + HALO + i
+
+    def joined(low, high, group):
+        return jnp.where(front, low, high) if group == 0 else jnp.where(front, high, low)
+
+    def sunshine_of(group):
+        lit = jnp.zeros((half, lanes), jnp.int32)
+        for slot in range(half):
+            lit = jnp.where(sublane == slot, sunlit[0, row_of(slot, group)], lit)
+        sun = insolation[...].astype(F32)
+        return jnp.where(lit == 1, joined(sun[:half], sun[half:], group), 0.0)
 
     def radiate(group):
         for copy in copies[group]:
@@ -153,21 +165,19 @@
             pair = depth_in[pl.ds(row * per_tile, 2 * per_tile), :].astype(F32)
             depth_f[pl.ds(slot * depth_step, per_tile), :] = pair[:per_tile]
             depth_f[pl.ds((slot + 1) * depth_step, per_tile), :] = pair[per_tile:]
-        for slot in range(8):
-            albedo_f[pl.ds(slot * level_step, levels), :] = albedo_in[row_of(slot, group)].astype(F32)
-            albedo_f[pl.ds(slot * level_step + levels, 1), :] = jnp.zeros((1, lanes), F32)
-
         def depth_at(level, g):
             return depth_f[pl.ds(level * points + g, 8, stride=depth_step), :]
 
         def albedo_at(level):
-            return albedo_f[pl.ds(level, 8, stride=level_step), :]
+            pair = albedo_in[pl.ds(pl.multiple_of(level * rows, rows), rows), :].astype(F32)
+            return joined(pair[:half], pair[half:], group)
 
         def down(step, carry):
             for inner in range(UNROLL):
                 level = step * UNROLL + inner
                 albedo_now, link_prev, state = carry
-                albedo_next = albedo_at(level + 1)
+                albedo_next = albedo_at(jnp.minimum(level + 1, levels - 1))
+                albedo_next = jnp.where(level + 1 < levels, albedo_next, 0.0)
                 link = albedo_now * albedo_next
                 base = base_loss + link_prev + link
                 lost = 2.0 - 2.0 * albedo_now
@@ -197,7 +207,7 @@
         start = (albedo_at(0), zero, tuple((zero, one, one, zero, zero) for _ in range(points)))
         lax.fori_loop(0, levels // UNROLL, down, start)
 
-        sunshine = sun[pl.ds(8 * group, 8), :]
+        sunshine = sunshine_of(group)
 
         def up(step, flux):
             for inner in range(UNROLL):
@@ -210,37 +220,44 @@
                     later.append(now)
                 flux = tuple(later)
                 heat = (sunshine - sunshine * albedo_at(level)) * (plain[level] + absorbed)
-                heat_f[pl.ds(level, 8, stride=level_step), :] = heat
+                at = pl.multiple_of(level * rows, rows)
+                low, high = pl.ds(at, half), pl.ds(pl.multiple_of(at + half, half), half)
+                start = joined(anomaly_in[low, :], anomaly_in[high, :], group)
+                field[pl.ds(half * group * slab + level, half, stride=slab), :] = heat + start
+                if group == 0:
+                    heat_held[level] = heat
+                else:
+                    other = heat_held[level]
+                    heat_out[low, :] = jnp.where(front, other, heat)
+                    heat_out[high, :] = jnp.where(front, heat, other)
             return flux
 
         lax.fori_loop(0, levels // UNROLL, up, tuple(zero for _ in range(points)))
-        for slot in range(8):
-            row = row_of(slot, group)
-            heat = heat_f[pl.ds(slot * level_step, levels), :]
-            heat_out[row] = heat
-            field[HALO + row] = heat + anomaly_in[row]
 
     def by_levels(body):
         def step(j, _):
-            body(pl.ds(pl.multiple_of(j * 8, 8), 8))
+            body(pl.multiple_of(j * 8, 8))
             return 0
 
         lax.fori_loop(0, levels // 8, step, 0)
         if levels % 8:
-            body(pl.ds(levels - 8, 8))
+            body(levels - 8)
+
+    def row_levels(row, first):
+        return field[pl.ds(places[row] * slab + first, 8), :]
 
     lane = lax.broadcasted_iota(jnp.int32, (8, lanes), 1)
     lane_row, lane_edge = lane // EDGE, lane % EDGE
 
-    def gather_edges(start, wanted, span):
+    def gather_edges(start, wanted, first):
         value = start
-        for place, index in wanted:
-            moved = pltpu.roll(field[index, span, :], (place * EDGE + HALO) % lanes, 1)
+        for place, row in wanted:
+            moved = pltpu.roll(row_levels(row, first), (place * EDGE + HALO) % lanes, 1)
             value = jnp.where(lane_row == place, moved, value)
         return value
 
-    outer = [(r, HALO + r) for r in (*range(HALO), *range(rows - HALO, rows))]
-    inner = [(r, HALO + r) for r in range(HALO, rows - HALO)]
+    outer = [(r, r) for r in (*range(HALO), *range(rows - HALO, rows))]
+    inner = [(r, r) for r in range(HALO, rows - HALO)]
 
     def remote(source, target, number, to_tile, to_band):
         return pltpu.make_async_remote_copy(
@@ -248,8 +265,11 @@
             device_id=(to_tile, to_band), device_id_type=MESH,
         )
 
-    to_north = [remote(field.at[pl.ds(HALO, HALO)], field.at[pl.ds(HALO + rows, HALO)], 0, north, band)]
-    to_south = [remote(field.at[pl.ds(rows, HALO)], field.at[pl.ds(0, HALO)], 1, south, band)]
+    def slabs(first_row):
+        return field.at[pl.ds(places[first_row] * slab, HALO * slab)]
+
+    to_north = [remote(slabs(0), slabs(rows), 0, north, band)]
+    to_south = [remote(slabs(rows - HALO), slabs(-HALO), 1, south, band)]
     to_side = []
     for j, side in enumerate(sides):
         to_north.append(remote(corner, got_corner.at[0, j], 2 + 3 * j, north, side))
@@ -259,8 +279,8 @@
     anomaly_copy.wait()
     radiate(0)
 
-    def pack_outer(span):
-        corner[span, :] = gather_edges(jnp.zeros((8, lanes), F32), outer, span)
+    def pack_outer(first):
+        corner[pl.ds(first, 8), :] = gather_edges(jnp.zeros((8, lanes), F32), outer, first)
 
     by_levels(pack_outer)
 
@@ -279,20 +299,21 @@
 
     @pl.when(jnp.logical_not(has_north))
     def _():
-        field[pl.ds(0, HALO)] = jnp.zeros((HALO, levels, lanes), F32)
+        slabs(-HALO)[...] = jnp.zeros((HALO * slab, lanes), F32)
         for j in range(n_sides):
             got_corner[1, j] = jnp.zeros((levels, lanes), F32)
 
     @pl.when(jnp.logical_not(has_south))
     def _():
-        field[pl.ds(HALO + rows, HALO)] = jnp.zeros((HALO, levels, lanes), F32)
+        slabs(rows)[...] = jnp.zeros((HALO * slab, lanes), F32)
         for j in range(n_sides):
             got_corner[0, j] = jnp.zeros((levels, lanes), F32)
 
     radiate(1)
 
-    def pack_inner(span):
-        strip[span, :] = gather_edges(corner[span, :], inner, span)
+    def pack_inner(first):
+        span = pl.ds(first, 8)
+        strip[span, :] = gather_edges(corner[span, :], inner, first)
 
     by_levels(pack_inner)
     for copy in to_side:
@@ -314,8 +335,8 @@
     keep_south = jnp.where(has_south, 1.0, 0.0).astype(F32)
     full = rows + 2 * HALO
 
-    def diffuse(span):
-        now = [field[i, span, :] for i in range(full)]
+    def diffuse(first):
+        now = [row_levels(i - HALO, first) for i in range(full)]
         for sweep in range(1, DIFF_STEPS + 1):
             later = [None] * full
             for i in range(sweep, full - sweep):
@@ -328,7 +349,7 @@
                 later[i] = value
             now = later
         for r in range(rows):
-            smooth[r, span, :] = now[HALO + r] * (mixing_rate**DIFF_STEPS)
+            smooth[pl.ds(r * smooth_step + first, 8), :] = now[HALO + r] * (mixing_rate**DIFF_STEPS)
 
     by_levels(diffuse)
 
@@ -342,10 +363,11 @@
             return west
         return jnp.where(lane_edge < HALO, west, ref[(*lead, 1, span, slice(None))])
 
-    beyond = [(rows - HALO + i, i) for i in range(HALO)] + [(i, HALO + rows + i) for i in range(HALO)]
-
-    def differ(span):
-        here = gather_edges(jnp.zeros((8, lanes), F32), beyond, span)
+    beyond = [(rows - HALO + i, i - HALO) for i in range(HALO)] + [(i, rows + i) for i in range(HALO)]
+
+    def differ(first):
+        span = pl.ds(first, 8)
+        here = gather_edges(jnp.zeros((8, lanes), F32), beyond, first)
         there = jnp.where(
             lane_row < HALO,
             pick(got_corner, span, 0),
@@ -353,32 +375,34 @@
         )
         return jnp.concatenate([pick(got, span) - strip[span, :], there - here], axis=1)
 
-    def correct(span):
+    def correct(first, fresh):
         fix = jnp.dot(
-            differ(span), mats[...], precision=lax.Precision.HIGHEST, preferred_element_type=F32
+            differ(first), mats[...], precision=lax.Precision.HIGHEST, preferred_element_type=F32
         )
         for r in range(rows):
-            moved = pltpu.roll(jnp.where(lane_row == r, fix, 0.0), (2 * lanes - r * EDGE - HALO) % lanes, 1)
-            smooth[r, span, :] = smooth[r, span, :] + moved
-
-    def correct_last(span):
-        fix = jnp.dot(
-            differ(span), mats[...], precision=lax.Precision.HIGHEST, preferred_element_type=F32
-        )
-        fresh = lax.broadcasted_iota(jnp.int32, (8, lanes), 0) >= 8 - levels % 8
-        for r in range(rows):
-            chosen = jnp.where((lane_row == r) & fresh, fix, 0.0)
-            moved = pltpu.roll(chosen, (2 * lanes - r * EDGE - HALO) % lanes, 1)
-            smooth[r, span, :] = smooth[r, span, :] + moved
+            chosen = lane_row == r if fresh is None else (lane_row == r) & fresh
+            moved = pltpu.roll(jnp.where(chosen, fix, 0.0), (2 * lanes - r * EDGE - HALO) % lanes, 1)
+            span = pl.ds(r * smooth_step + first, 8)
+            smooth[span, :] = smooth[span, :] + moved
 
     def correct_step(j, _):
-        correct(pl.ds(pl.multiple_of(j * 8, 8), 8))
+        correct(pl.multiple_of(j * 8, 8), None)
         return 0
 
     lax.fori_loop(0, levels // 8, correct_step, 0)
     if levels % 8:
-        correct_last(pl.ds(levels - 8, 8))
-    smooth_copy = pltpu.make_async_copy(smooth, smooth_hbm, out_sem.at[1])
+        correct(levels - 8, sublane >= 8 - levels % 8)
+
+    def put_back(step, _):
+        for inner in range(UNROLL):
+            level = step * UNROLL + inner
+            for part in range(2):
+                value = smooth[pl.ds(part * half * smooth_step + level, half, stride=smooth_step), :]
+                smooth_out[pl.ds(pl.multiple_of(level * rows + part * half, half), half), :] = value
+        return 0
+
+    lax.fori_loop(0, levels // UNROLL, put_back, 0)
+    smooth_copy = pltpu.make_async_copy(smooth_out, smooth_hbm, out_sem.at[1])
     smooth_copy.start()
 
     @pl.when(has_north)
@@ -401,30 +425,33 @@
     rows, levels, points, lanes = optical_depth.shape
     n_sides = 1 if n_band == 2 else 2
     mats = edge_weights(rows)
-    level_step = (levels + 7) // 8 * 8 + 1
-    shape = jax.ShapeDtypeStruct((rows, levels, lanes), F32)
+    slab = (levels + 7) // 8 * 8 + 2
+
+    def by_level(x):
+        return jnp.swapaxes(x, 0, 1).reshape(levels * rows, lanes)
+
+    shape = jax.ShapeDtypeStruct((levels * rows, lanes), F32)
     vmem, smem, hbm = (pl.BlockSpec(memory_space=m) for m in (pltpu.VMEM, pltpu.SMEM, pl.ANY))
     n_copies = 2 + 3 * n_sides
-    return pl.pallas_call(
+    heating, smoothed = pl.pallas_call(
         functools.partial(kernel, n_tiles, n_band, rows, levels, points),
         out_shape=(shape, shape),
-        in_specs=[hbm, hbm, hbm, hbm, vmem, vmem, smem],
+        in_specs=[hbm, hbm, hbm, hbm, vmem, smem, smem],
         out_specs=(hbm, hbm),
         scratch_shapes=[
             pltpu.VMEM((rows * levels * points, lanes), jnp.bfloat16),
-            pltpu.VMEM((rows, levels, lanes), jnp.bfloat16),
-            pltpu.VMEM((rows, levels, lanes), F32),
+            pltpu.VMEM((levels * rows, lanes), jnp.bfloat16),
+            pltpu.VMEM((levels * rows, lanes), F32),
             pltpu.VMEM(mats.shape[1:], F32),
-            pltpu.VMEM((rows, lanes), F32),
             pltpu.VMEM((8 * (levels * points + 1), lanes), F32),
-            pltpu.VMEM((8 * level_step, lanes), F32),
             pltpu.VMEM((levels, points, 8, lanes), F32),
             pltpu.VMEM((levels, points, 8, lanes), F32),
             pltpu.VMEM((levels, 8, lanes), F32),
-            pltpu.VMEM((8 * level_step, lanes), F32),
-            pltpu.VMEM((rows, levels, lanes), F32),
-            pltpu.VMEM((rows + 2 * HALO, levels, lanes), F32),
-            pltpu.VMEM((rows, levels, lanes), F32),
+            pltpu.VMEM((levels, 8, lanes), F32),
+            pltpu.VMEM((levels * rows, lanes), F32),
+            pltpu.VMEM(((rows + 2 * HALO) * slab, lanes), F32),
+            pltpu.VMEM((rows * (slab - 1), lanes), F32),
+            pltpu.VMEM((levels * rows, lanes), F32),
             pltpu.VMEM((levels, lanes), F32),
             pltpu.VMEM((levels, lanes), F32),
             pltpu.VMEM((n_sides, levels, lanes), F32),
@@ -435,12 +462,13 @@
             pltpu.SemaphoreType.DMA((n_copies,)),
         ],
         compiler_params=pltpu.CompilerParams(
-            collective_id=0, has_side_effects=True, vmem_limit_bytes=40 * 1024 * 1024
+            collective_id=0, has_side_effects=True, vmem_limit_bytes=56 * 1024 * 1024
         ),
     )(
-        optical_depth.reshape(rows * levels * points, lanes), albedo, anomaly, jnp.asarray(mats),
-        insolation, sunlit, point_weight,
+        optical_depth.reshape(rows * levels * points, lanes),
+        by_level(albedo), by_level(anomaly), jnp.asarray(mats), insolation, sunlit.T, point_weight,
     )
+    return tuple(jnp.swapaxes(x.reshape(levels, rows, lanes), 0, 1) for x in (heating, smoothed))
 
 
 def solution(mesh):

time: 27.2 us -> 25.3 us (0.930)
  local copies, waits for them, and re-layouts: 5.92 us -> 2.96 us
  Pallas kernels: 20.4 us -> 21.5 us
    pallas_call x2 -> x0, local copies, waits for them, and re-layouts: 2.59 us -> none  [per_device(): pl.pallas_call(functools.partial(kernel, n_tiles, n_band, rows, levels, p...]
    pallas_call x1, Pallas kernels: 20.4 us -> 21.5 us  [per_device(): pl.pallas_call(functools.partial(kernel, n_tiles, n_band, rows, levels, p...]
    unnamed x11 -> x4, local copies, waits for them, and re-layouts: 3.33 us -> 2.96 us
where the time goes in v2:
time: 25.3 us; the launch traced here: 25.1 us
  Pallas kernels  21.5 us (85%)
  local copies, waits for them, and re-layouts  2.96 us (12%)
  between operations  0.65 us (3%)
    pallas_call x1, Pallas kernels, per_device(): pl.pallas_call(functools.partial(kernel, n_tiles, n_band, rows, levels, p...  21.5 us
    unnamed x4, local copies, waits for them, and re-layouts  2.96 us

profile of v2, /device:TPU:9, one launch (start us, length us, event | category | flops | bytes accessed | tf_op | source)
XLA Modules:
  0.0 25.1 jit_solution(10253087165181265069)
XLA Ops:
  0.6 21.5 %shard_map.86 = (f32[1440,128]{1,0:T(8,128)}, f32[1440,128]{1,0:T(8,128)}) custom-call(bf16[5760,128]{1,0:T(8,128)(2,1)} %bitcast.14, bf16[1440,128]{1,0:T(8,128)(2,1)} %bitcast.18, f32[1440,128]{1,0:T(8,128)} %bitcast.15, f32[4,256,128]{2,1,0:T(8,128)} %constant.2.clone.mats_hbm, bf16[16,128]{1,0:T(8,128)(2,1)} %insolation.1, s32[1,16]{1,0:T(1,128)} %bitcast.19, ...), custom_call_target="tpu_custom_call" | custom-call | tf_op jit(solution)/shard_map/pallas_call | solution.py:436
  22.1 0.0 copy-start
  22.2 2.1 %copy.11 = f32[16,90,128]{2,0,1:T(8,128)} copy(f32[16,90,128]{2,0,1:T(8,128)} %bitcast.17) | data formatting | bytes 1474560
  24.3 0.0 copy-done
  24.3 0.9 %copy.12 = f32[16,90,128]{2,0,1:T(8,128)} copy(f32[16,90,128]{2,0,1:T(8,128)S(1)} %bitcast.16) | data formatting | bytes 1474560
Async XLA Ops:
  22.1 2.1 %copy-start = (f32[1440,128]{1,0:T(8,128)S(1)}, f32[1440,128]{1,0:T(8,128)}, u32[]{:S(2)}) copy-start(f32[1440,128]{1,0:T(8,128)} %get-tuple-element.5) | copy-start | bytes 2211844

commit v3 on v2

--- a/solution.py
+++ b/solution.py
@@ -13,6 +13,7 @@
 HALO = 4
 EDGE = 2 * HALO
 UNROLL = 9
+CHUNK = 24
 
 mixing_rate = 0.2
 base_loss = 0.005
@@ -51,28 +52,28 @@
                     gap = abs(q_to - q_from)
                     if gap > reach:
                         continue
-                    weight = columns[reach][reach + gap] * mixing_rate**DIFF_STEPS
+                    weight = columns[reach][reach + gap]
                     for r_to in range(rows):
                         for r_from in range(full):
                             if r_from < HALO:
-                                lane = rows * EDGE + (rows - HALO + r_from) * EDGE
+                                lane = (rows + r_from) * EDGE
                             elif r_from < HALO + rows:
                                 lane = (r_from - HALO) * EDGE
                             else:
-                                lane = rows * EDGE + (r_from - HALO - rows) * EDGE
+                                lane = r_from * EDGE
                             out[variant, lane + q_from, r_to * EDGE + q_to] += (
                                 weight * power[HALO + r_to, r_from]
                             )
-    return out.astype(np.float32)
+    return out.astype(jnp.bfloat16)
 
 
 def kernel(
     n_tiles, n_band, rows, levels, points,
     depth_hbm, albedo_hbm, anomaly_hbm, mats_hbm, insolation, sunlit, weight,
-    heat_hbm, smooth_hbm,
+    heat_out, smooth, fix,
     depth_in, albedo_in, anomaly_in, mats, depth_f, swept, ratio, plain, heat_held,
-    heat_out, field, smooth, smooth_out, strip, corner, got, got_corner,
-    in_sem, out_sem, send_sem, recv_sem,
+    field, strip, corner, got, got_corner, differ,
+    in_sem, send_sem, recv_sem,
 ):
     lanes = field.shape[1]
     half = rows // 2
@@ -256,6 +257,7 @@
             value = jnp.where(lane_row == place, moved, value)
         return value
 
+    blocks = [*range(0, levels - 7, 8)] + ([levels - 8] if levels % 8 else [])
     outer = [(r, r) for r in (*range(HALO), *range(rows - HALO, rows))]
     inner = [(r, r) for r in range(HALO, rows - HALO)]
 
@@ -272,17 +274,25 @@
     to_south = [remote(slabs(rows - HALO), slabs(-HALO), 1, south, band)]
     to_side = []
     for j, side in enumerate(sides):
-        to_north.append(remote(corner, got_corner.at[0, j], 2 + 3 * j, north, side))
-        to_south.append(remote(corner, got_corner.at[1, j], 3 + 3 * j, south, side))
+        to_north.append(remote(corner.at[0], got_corner.at[0, j], 2 + 3 * j, north, side))
+        to_south.append(remote(corner.at[1], got_corner.at[1, j], 3 + 3 * j, south, side))
         to_side.append(remote(strip, got.at[j], 4 + 3 * j, tile, side))
 
     anomaly_copy.wait()
     radiate(0)
 
-    def pack_outer(first):
-        corner[pl.ds(first, 8), :] = gather_edges(jnp.zeros((8, lanes), F32), outer, first)
-
-    by_levels(pack_outer)
+    def pack_corner(first_row):
+        packed = []
+        for j, first in enumerate(blocks):
+            if j % HALO == 0:
+                packed.append(jnp.zeros((8, lanes), F32))
+            wanted = [(j % HALO * HALO + i, first_row + i) for i in range(HALO)]
+            packed[-1] = gather_edges(packed[-1], wanted, first)
+        return packed
+
+    for end, first_row in enumerate((0, rows - HALO)):
+        for v, value in enumerate(pack_corner(first_row)):
+            corner[end, v] = value
 
     peers = n_sides + (1 + n_sides) * (has_north.astype(jnp.int32) + has_south.astype(jnp.int32))
     pl.semaphore_wait(barrier, peers)
@@ -301,25 +311,26 @@
     def _():
         slabs(-HALO)[...] = jnp.zeros((HALO * slab, lanes), F32)
         for j in range(n_sides):
-            got_corner[1, j] = jnp.zeros((levels, lanes), F32)
+            got_corner[1, j] = jnp.zeros(corner.shape[1:], F32)
 
     @pl.when(jnp.logical_not(has_south))
     def _():
         slabs(rows)[...] = jnp.zeros((HALO * slab, lanes), F32)
         for j in range(n_sides):
-            got_corner[0, j] = jnp.zeros((levels, lanes), F32)
-
-    radiate(1)
+            got_corner[0, j] = jnp.zeros(corner.shape[1:], F32)
+
+    def pack_outer(first):
+        strip[pl.ds(first, 8), :] = gather_edges(jnp.zeros((8, lanes), F32), outer, first)
 
     def pack_inner(first):
         span = pl.ds(first, 8)
-        strip[span, :] = gather_edges(corner[span, :], inner, first)
-
+        strip[span, :] = gather_edges(strip[span, :], inner, first)
+
+    by_levels(pack_outer)
+    radiate(1)
     by_levels(pack_inner)
     for copy in to_side:
         copy.start()
-    heat_copy = pltpu.make_async_copy(heat_out, heat_hbm, out_sem.at[0])
-    heat_copy.start()
 
     @pl.when(has_north)
     def _():
@@ -357,53 +368,32 @@
     for copy in to_side:
         copy.wait_recv()
 
-    def pick(ref, span, *lead):
-        west = ref[(*lead, 0, span, slice(None))]
+    def pick(ref, *at):
+        west = ref[(*at[:-1], 0, at[-1])]
         if n_sides == 1:
             return west
-        return jnp.where(lane_edge < HALO, west, ref[(*lead, 1, span, slice(None))])
-
-    beyond = [(rows - HALO + i, i - HALO) for i in range(HALO)] + [(i, rows + i) for i in range(HALO)]
-
-    def differ(first):
+        return jnp.where(lane_edge < HALO, west, ref[(*at[:-1], 1, at[-1])])
+
+    ends = []
+    for end, first_row in ((1, -HALO), (0, rows)):
+        ends.append([pick(got_corner, end, v) - here for v, here in enumerate(pack_corner(first_row))])
+    differ[pl.ds(differ.shape[0] - 8, 8), :] = jnp.zeros((8, 2 * lanes), F32)
+    width = HALO * EDGE
+    for j, first in enumerate(blocks):
         span = pl.ds(first, 8)
-        here = gather_edges(jnp.zeros((8, lanes), F32), beyond, first)
-        there = jnp.where(
-            lane_row < HALO,
-            pick(got_corner, span, 0),
-            jnp.where(lane_row >= rows - HALO, pick(got_corner, span, 1), 0.0),
-        )
-        return jnp.concatenate([pick(got, span) - strip[span, :], there - here], axis=1)
-
-    def correct(first, fresh):
-        fix = jnp.dot(
-            differ(first), mats[...], precision=lax.Precision.HIGHEST, preferred_element_type=F32
-        )
-        for r in range(rows):
-            chosen = lane_row == r if fresh is None else (lane_row == r) & fresh
-            moved = pltpu.roll(jnp.where(chosen, fix, 0.0), (2 * lanes - r * EDGE - HALO) % lanes, 1)
-            span = pl.ds(r * smooth_step + first, 8)
-            smooth[span, :] = smooth[span, :] + moved
-
-    def correct_step(j, _):
-        correct(pl.multiple_of(j * 8, 8), None)
-        return 0
-
-    lax.fori_loop(0, levels // 8, correct_step, 0)
-    if levels % 8:
-        correct(levels - 8, sublane >= 8 - levels % 8)
-
-    def put_back(step, _):
-        for inner in range(UNROLL):
-            level = step * UNROLL + inner
-            for part in range(2):
-                value = smooth[pl.ds(part * half * smooth_step + level, half, stride=smooth_step), :]
-                smooth_out[pl.ds(pl.multiple_of(level * rows + part * half, half), half), :] = value
-        return 0
-
-    lax.fori_loop(0, levels // UNROLL, put_back, 0)
-    smooth_copy = pltpu.make_async_copy(smooth_out, smooth_hbm, out_sem.at[1])
-    smooth_copy.start()
+        differ[span, pl.ds(0, lanes)] = pick(got, span) - strip[span, :]
+        above, below = (x[j // HALO] for x in ends)
+        above = pltpu.roll(above, (lanes - j % HALO * width) % lanes, 1)
+        below = pltpu.roll(below, (lanes + width - j % HALO * width) % lanes, 1)
+        beyond = jnp.where(lane < width, above, jnp.where(lane < 2 * width, below, 0.0))
+        differ[span, pl.ds(lanes, lanes)] = beyond
+    rest, total = differ[...], None
+    for _ in range(3):
+        part = rest.astype(jnp.bfloat16)
+        rest = rest - part.astype(F32)
+        term = jnp.dot(part, mats[...], preferred_element_type=F32)
+        total = term if total is None else total + term
+    fix[...] = total * (mixing_rate**DIFF_STEPS)
 
     @pl.when(has_north)
     def _():
@@ -417,8 +407,35 @@
 
     for copy in to_side:
         copy.wait_send()
-    heat_copy.wait()
-    smooth_copy.wait()
+
+
+def finish(rows, levels, heat, smooth, fix, heat_hbm, smooth_hbm, fixed, ordered, sem):
+    lanes = heat.shape[1]
+    half = rows // 2
+    step = smooth.shape[0] // rows
+    heat_copy = pltpu.make_async_copy(heat, heat_hbm, sem.at[0])
+    heat_copy.start()
+    lane_row = lax.broadcasted_iota(jnp.int32, (8, lanes), 1) // EDGE
+    copies, done = [heat_copy], 0
+    for first in [*range(0, levels - 7, 8)] + ([levels - 8] if levels % 8 else []):
+        value = fix[pl.ds(first, 8), :]
+        for r in range(rows):
+            moved = pltpu.roll(jnp.where(lane_row == r, value, 0.0), (2 * lanes - r * EDGE - HALO) % lanes, 1)
+            span = pl.ds(r * step + first, 8)
+            fixed[span, :] = smooth[span, :] + moved
+        if first + 8 - done < CHUNK and first + 8 < levels:
+            continue
+        for level in range(done, first + 8):
+            for part in range(2):
+                eight = fixed[pl.ds(part * half * step + level, half, stride=step), :]
+                ordered[pl.ds(level * rows + part * half, half), :] = eight
+        span = pl.ds(done * rows, (first + 8 - done) * rows)
+        copy = pltpu.make_async_copy(ordered.at[span], smooth_hbm.at[span], sem.at[len(copies)])
+        copy.start()
+        copies.append(copy)
+        done = first + 8
+    for copy in copies:
+        copy.wait()
 
 
 def per_device(n_tiles, n_band, optical_depth, albedo, insolation, sunlit, point_weight, anomaly):
@@ -431,43 +448,57 @@
         return jnp.swapaxes(x, 0, 1).reshape(levels * rows, lanes)
 
     shape = jax.ShapeDtypeStruct((levels * rows, lanes), F32)
-    vmem, smem, hbm = (pl.BlockSpec(memory_space=m) for m in (pltpu.VMEM, pltpu.SMEM, pl.ANY))
+    vmem, smem, hbm = (pl.BlockSpec(memory_space=m) for m in (pltpu.VMEM, pltpu.SMEM, pltpu.HBM))
     n_copies = 2 + 3 * n_sides
-    heating, smoothed = pl.pallas_call(
+    deep = (levels + 7) // 8 * 8
+    heat, smooth, fix = pl.pallas_call(
         functools.partial(kernel, n_tiles, n_band, rows, levels, points),
-        out_shape=(shape, shape),
+        out_shape=(
+            shape,
+            jax.ShapeDtypeStruct((rows * (slab - 1), lanes), F32),
+            jax.ShapeDtypeStruct((deep, lanes), F32),
+        ),
         in_specs=[hbm, hbm, hbm, hbm, vmem, smem, smem],
-        out_specs=(hbm, hbm),
+        out_specs=(vmem, vmem, vmem),
         scratch_shapes=[
             pltpu.VMEM((rows * levels * points, lanes), jnp.bfloat16),
             pltpu.VMEM((levels * rows, lanes), jnp.bfloat16),
             pltpu.VMEM((levels * rows, lanes), F32),
-            pltpu.VMEM(mats.shape[1:], F32),
+            pltpu.VMEM(mats.shape[1:], jnp.bfloat16),
             pltpu.VMEM((8 * (levels * points + 1), lanes), F32),
             pltpu.VMEM((levels, points, 8, lanes), F32),
             pltpu.VMEM((levels, points, 8, lanes), F32),
             pltpu.VMEM((levels, 8, lanes), F32),
             pltpu.VMEM((levels, 8, lanes), F32),
-            pltpu.VMEM((levels * rows, lanes), F32),
             pltpu.VMEM(((rows + 2 * HALO) * slab, lanes), F32),
-            pltpu.VMEM((rows * (slab - 1), lanes), F32),
-            pltpu.VMEM((levels * rows, lanes), F32),
             pltpu.VMEM((levels, lanes), F32),
-            pltpu.VMEM((levels, lanes), F32),
+            pltpu.VMEM((2, deep // 32, 8, lanes), F32),
             pltpu.VMEM((n_sides, levels, lanes), F32),
-            pltpu.VMEM((2, n_sides, levels, lanes), F32),
+            pltpu.VMEM((2, n_sides, deep // 32, 8, lanes), F32),
+            pltpu.VMEM((deep, 2 * lanes), F32),
             pltpu.SemaphoreType.DMA((8,)),
-            pltpu.SemaphoreType.DMA((2,)),
             pltpu.SemaphoreType.DMA((n_copies,)),
             pltpu.SemaphoreType.DMA((n_copies,)),
         ],
         compiler_params=pltpu.CompilerParams(
-            collective_id=0, has_side_effects=True, vmem_limit_bytes=56 * 1024 * 1024
+            collective_id=0, has_side_effects=True, vmem_limit_bytes=20 * 1024 * 1024
         ),
     )(
         optical_depth.reshape(rows * levels * points, lanes),
         by_level(albedo), by_level(anomaly), jnp.asarray(mats), insolation, sunlit.T, point_weight,
     )
+    heating, smoothed = pl.pallas_call(
+        functools.partial(finish, rows, levels),
+        out_shape=(shape, shape),
+        in_specs=[vmem, vmem, vmem],
+        out_specs=(hbm, hbm),
+        scratch_shapes=[
+            pltpu.VMEM((rows * (slab - 1), lanes), F32),
+            pltpu.VMEM((levels * rows, lanes), F32),
+            pltpu.SemaphoreType.DMA((2 + levels // CHUNK + 1,)),
+        ],
+        compiler_params=pltpu.CompilerParams(vmem_limit_bytes=20 * 1024 * 1024),
+    )(heat, smooth, fix)
     return tuple(jnp.swapaxes(x.reshape(levels, rows, lanes), 0, 1) for x in (heating, smoothed))
 
 

time: 25.3 us -> 23.7 us (0.937)
  Pallas kernels: 21.5 us -> 16.4 us
  local copies, waits for them, and re-layouts: 2.96 us -> 6.41 us
    pallas_call x1, Pallas kernels: 21.5 us -> 15.2 us  [per_device(): pl.pallas_call(functools.partial(kernel, n_tiles, n_band, rows, levels, p...]
    unnamed x4 -> x14, local copies, waits for them, and re-layouts: 2.96 us -> 6.41 us
    pallas_call x0 -> x1, Pallas kernels: none -> 1.15 us  [per_device(): pl.pallas_call(functools.partial(finish, rows, levels), out_shape=(shape,...]
where the time goes in v3:
time: 23.7 us; the launch traced here: 23.4 us
  Pallas kernels  16.4 us (69%)
  local copies, waits for them, and re-layouts  6.41 us (27%)
  between operations  0.65 us (3%)
    pallas_call x1, Pallas kernels, per_device(): pl.pallas_call(functools.partial(kernel, n_tiles, n_band, rows, levels, p...  15.2 us
    unnamed x14, local copies, waits for them, and re-layouts  6.41 us
    pallas_call x1, Pallas kernels, per_device(): pl.pallas_call(functools.partial(finish, rows, levels), out_shape=(shape,...  1.15 us

profile of v3, /device:TPU:9, one launch (start us, length us, event | category | flops | bytes accessed | tf_op | source)
XLA Modules:
  0.0 23.4 jit_solution(8679581973557855147)
XLA Ops:
  0.6 0.0 copy-start
  0.6 1.4 %copy-done = bf16[16,90,4,128]{3,2,1,0:T(4,128)(2,1)S(1)} copy-done((bf16[16,90,4,128]{3,2,1,0:T(4,128)(2,1)S(1)}, bf16[16,90,4,128]{3,2,1,0:T(4,128)(2,1)}, u32[]{:S(2)}) %copy-start) | copy-done | bytes 1474584
  2.0 0.0 copy-start.1
  2.0 1.1 %copy-done.1 = f32[16,90,128]{2,0,1:T(8,128)S(1)} copy-done((f32[16,90,128]{2,0,1:T(8,128)S(1)}, f32[16,90,128]{2,0,1:T(8,128)}, u32[]{:S(2)}) %copy-start.1) | copy-done | bytes 737304
  3.1 0.0 copy-start.2
  3.1 1.0 %copy-done.2 = bf16[16,90,128]{2,0,1:T(8,128)(2,1)S(1)} copy-done((bf16[16,90,128]{2,0,1:T(8,128)(2,1)S(1)}, bf16[16,90,128]{2,0,1:T(8,128)(2,1)}, u32[]{:S(2)}) %copy-start.2) | copy-done | bytes 368664
  4.1 0.0 copy-start.3
  4.1 0.9 %copy-done.3 = bf16[4,256,128]{2,1,0:T(8,128)(2,1)S(1)} copy-done((bf16[4,256,128]{2,1,0:T(8,128)(2,1)S(1)}, bf16[4,256,128]{2,1,0:T(8,128)(2,1)}, u32[]{:S(2)}) %copy-start.3) | copy-done | bytes 262168
  5.1 0.0 copy-start.4
  5.1 0.7 %copy-done.4 = bf16[16,128]{1,0:T(8,128)(2,1)S(1)} copy-done((bf16[16,128]{1,0:T(8,128)(2,1)S(1)}, bf16[16,128]{1,0:T(8,128)(2,1)}, u32[]{:S(2)}) %copy-start.4) | copy-done | bytes 4120
  5.7 0.0 copy-start.5
  5.8 0.7 %copy-done.5 = s32[16,1]{0,1:T(1,128)S(1)} copy-done((s32[16,1]{0,1:T(1,128)S(1)}, s32[16,1]{0,1:T(1,128)}, u32[]{:S(2)}) %copy-start.5) | copy-done | bytes 88
  6.4 0.0 copy-start.6
  6.4 0.7 %copy-done.6 = f32[4]{0:T(128)S(1)} copy-done((f32[4]{0:T(128)S(1)}, f32[4]{0:T(128)}, u32[]{:S(2)}) %copy-start.6) | copy-done | bytes 40
  7.1 15.2 %shard_map.86 = (f32[1440,128]{1,0:T(8,128)S(1)}, f32[1552,128]{1,0:T(8,128)S(1)}, f32[96,128]{1,0:T(8,128)S(1)}) custom-call(bf16[5760,128]{1,0:T(8,128)(2,1)S(1)} %bitcast.14, bf16[1440,128]{1,0:T(8,128)(2,1)S(1)} %bitcast.16, f32[1440,128]{1,0:T(8,128)S(1)} %bitcast.15, bf16[4,256,128]{2,1,0:T(8,128)(2,1)S(1)} %copy-done.3, ...), custom_call_target="tpu_custom_call" | custom-call | tf_op jit(solution)/shard_map/pallas_call | solution.py:454
  22.3 1.2 %shard_map.87 = (f32[1440,128]{1,0:T(8,128)}, f32[1440,128]{1,0:T(8,128)}) custom-call(f32[1440,128]{1,0:T(8,128)S(1)} %get-tuple-element.7.heat, f32[1552,128]{1,0:T(8,128)S(1)} %get-tuple-element.8.smooth, f32[96,128]{1,0:T(8,128)S(1)} %get-tuple-element.9.fix), custom_call_target="tpu_custom_call" | custom-call | tf_op jit(solution)/shard_map/pallas_call | solution.py:490
Async XLA Ops:
  0.6 1.4 %copy-start = (bf16[16,90,4,128]{3,2,1,0:T(4,128)(2,1)S(1)}, bf16[16,90,4,128]{3,2,1,0:T(4,128)(2,1)}, u32[]{:S(2)}) copy-start(bf16[16,90,4,128]{3,2,1,0:T(4,128)(2,1)} %param.7) | copy-start | bytes 4423684
  2.0 1.1 %copy-start.1 = (f32[16,90,128]{2,0,1:T(8,128)S(1)}, f32[16,90,128]{2,0,1:T(8,128)}, u32[]{:S(2)}) copy-start(f32[16,90,128]{2,0,1:T(8,128)} %param.12) | copy-start | bytes 2211844
  3.1 1.0 %copy-start.2 = (bf16[16,90,128]{2,0,1:T(8,128)(2,1)S(1)}, bf16[16,90,128]{2,0,1:T(8,128)(2,1)}, u32[]{:S(2)}) copy-start(bf16[16,90,128]{2,0,1:T(8,128)(2,1)} %param.8) | copy-start | bytes 1105924
  4.1 0.9 %copy-start.3 = (bf16[4,256,128]{2,1,0:T(8,128)(2,1)S(1)}, bf16[4,256,128]{2,1,0:T(8,128)(2,1)}, u32[]{:S(2)}) copy-start(bf16[4,256,128]{2,1,0:T(8,128)(2,1)} %constant.2.clone.mats_hbm) | copy-start | bytes 786436
  5.1 0.7 %copy-start.4 = (bf16[16,128]{1,0:T(8,128)(2,1)S(1)}, bf16[16,128]{1,0:T(8,128)(2,1)}, u32[]{:S(2)}) copy-start(bf16[16,128]{1,0:T(8,128)(2,1)} %insolation.1) | copy-start | bytes 12292
  5.7 0.7 %copy-start.5 = (s32[16,1]{0,1:T(1,128)S(1)}, s32[16,1]{0,1:T(1,128)}, u32[]{:S(2)}) copy-start(s32[16,1]{0,1:T(1,128)} %param.10) | copy-start | bytes 196
  6.4 0.7 %copy-start.6 = (f32[4]{0:T(128)S(1)}, f32[4]{0:T(128)}, u32[]{:S(2)}) copy-start(f32[4]{0:T(128)} %weight.1) | copy-start | bytes 52

commit v4 on v3

--- a/solution.py
+++ b/solution.py
@@ -12,7 +12,8 @@
 DIFF_STEPS = 4
 HALO = 4
 EDGE = 2 * HALO
-UNROLL = 9
+UNROLL = 18
+TOGETHER = 3
 CHUNK = 24
 
 mixing_rate = 0.2
@@ -69,11 +70,11 @@
 
 def kernel(
     n_tiles, n_band, rows, levels, points,
-    depth_hbm, albedo_hbm, anomaly_hbm, mats_hbm, insolation, sunlit, weight,
-    heat_out, smooth, fix,
-    depth_in, albedo_in, anomaly_in, mats, depth_f, swept, ratio, plain, heat_held,
-    field, strip, corner, got, got_corner, differ,
-    in_sem, send_sem, recv_sem,
+    depth_hbm, albedo_hbm, anomaly_hbm, mats_hbm, insolation_hbm, sunlit_hbm, weight_hbm,
+    heat_hbm, smooth_hbm, fix_hbm,
+    depth_in, albedo_in, anomaly_in, mats, insolation, sunlit, weight, depth_f, swept, ratio, plain, heat_held,
+    heat_out, smooth, fix, field, strip, corner, got, got_corner, differ,
+    in_sem, out_sem, send_sem, recv_sem,
 ):
     lanes = field.shape[1]
     half = rows // 2
@@ -118,7 +119,7 @@
             span = pl.ds(first * per_tile, count * per_tile)
             mine.append((depth_hbm.at[span], depth_in.at[span]))
         loads.append(mine)
-    loads[0].append((albedo_hbm, albedo_in))
+    loads[0] += [(albedo_hbm, albedo_in), (insolation_hbm, insolation), (sunlit_hbm, sunlit), (weight_hbm, weight)]
     copies, number = [], 0
     for mine in loads:
         started = []
@@ -134,7 +135,6 @@
     mats_copy = pltpu.make_async_copy(mats_hbm.at[variant], mats, in_sem.at[number + 1])
     mats_copy.start()
 
-    weights = [weight[g] for g in range(points)]
     sublane = lax.broadcasted_iota(jnp.int32, (half, lanes), 0)
     front = sublane < HALO
 
@@ -161,6 +161,7 @@
     def radiate(group):
         for copy in copies[group]:
             copy.wait()
+        weights = [weight[g] for g in range(points)]
         for slot in range(0, 8, 2):
             row = row_of(slot, group)
             pair = depth_in[pl.ds(row * per_tile, 2 * per_tile), :].astype(F32)
@@ -186,11 +187,10 @@
                 for g in range(points):
                     total, beam, p, m, s = state[g]
                     layer = depth_at(level, g)
-                    total = total + layer
-                    beam_new = jnp.exp(total * -2.0)
+                    total = total + layer * exponent
+                    beam_new = weights[g] * jnp.exp2(total)
                     extinct = beam - beam_new
-                    term = weights[g] * extinct
-                    direct = term if direct is None else direct + term
+                    direct = extinct if direct is None else direct + extinct
                     p_new = (base + lost * layer) * p - link_prev * m
                     m_new = link * p
                     s_new = (albedo_now * extinct) * p + link_prev * s
@@ -203,9 +203,10 @@
                 carry = (albedo_next, link, tuple(later))
             return carry
 
+        exponent = -2.0 / math.log(2.0)
         zero = jnp.zeros((8, lanes), F32)
         one = jnp.ones((8, lanes), F32)
-        start = (albedo_at(0), zero, tuple((zero, one, one, zero, zero) for _ in range(points)))
+        start = (albedo_at(0), zero, tuple((zero, weights[g] * one, one, zero, zero) for g in range(points)))
         lax.fori_loop(0, levels // UNROLL, down, start)
 
         sunshine = sunshine_of(group)
@@ -216,11 +217,11 @@
                 later, absorbed = [], None
                 for g in range(points):
                     now = swept[level, g] + ratio[level, g] * flux[g]
-                    term = (2.0 * weights[g]) * depth_at(level, g) * now
+                    term = depth_at(level, g) * now
                     absorbed = term if absorbed is None else absorbed + term
                     later.append(now)
                 flux = tuple(later)
-                heat = (sunshine - sunshine * albedo_at(level)) * (plain[level] + absorbed)
+                heat = (sunshine - sunshine * albedo_at(level)) * (plain[level] + 2.0 * absorbed)
                 at = pl.multiple_of(level * rows, rows)
                 low, high = pl.ds(at, half), pl.ds(pl.multiple_of(at + half, half), half)
                 start = joined(anomaly_in[low, :], anomaly_in[high, :], group)
@@ -235,15 +236,6 @@
 
         lax.fori_loop(0, levels // UNROLL, up, tuple(zero for _ in range(points)))
 
-    def by_levels(body):
-        def step(j, _):
-            body(pl.multiple_of(j * 8, 8))
-            return 0
-
-        lax.fori_loop(0, levels // 8, step, 0)
-        if levels % 8:
-            body(levels - 8)
-
     def row_levels(row, first):
         return field[pl.ds(places[row] * slab + first, 8), :]
 
@@ -326,9 +318,13 @@
         span = pl.ds(first, 8)
         strip[span, :] = gather_edges(strip[span, :], inner, first)
 
-    by_levels(pack_outer)
+    for first in blocks:
+        pack_outer(first)
     radiate(1)
-    by_levels(pack_inner)
+    heat_copy = pltpu.make_async_copy(heat_out, heat_hbm, out_sem.at[0])
+    heat_copy.start()
+    for first in blocks:
+        pack_inner(first)
     for copy in to_side:
         copy.start()
 
@@ -346,23 +342,31 @@
     keep_south = jnp.where(has_south, 1.0, 0.0).astype(F32)
     full = rows + 2 * HALO
 
-    def diffuse(first):
-        now = [row_levels(i - HALO, first) for i in range(full)]
+    def sweep_rows(now, sweep):
+        later = [None] * full
+        for i in range(sweep, full - sweep):
+            x = now[i]
+            value = (x + pltpu.roll(x, 1, 1)) + (pltpu.roll(x, lanes - 1, 1) + (now[i - 1] + now[i + 1]))
+            if i < HALO:
+                value = value * keep_north
+            if i >= HALO + rows:
+                value = value * keep_south
+            later[i] = value
+        return later
+
+    def diffuse(step, _):
+        firsts = [jnp.minimum((step * TOGETHER + b) * 8, levels - 8) for b in range(TOGETHER)]
+        state = [[row_levels(i - HALO, first) for i in range(full)] for first in firsts]
         for sweep in range(1, DIFF_STEPS + 1):
-            later = [None] * full
-            for i in range(sweep, full - sweep):
-                x = now[i]
-                value = (x + pltpu.roll(x, 1, 1)) + (pltpu.roll(x, lanes - 1, 1) + (now[i - 1] + now[i + 1]))
-                if i < HALO:
-                    value = value * keep_north
-                if i >= HALO + rows:
-                    value = value * keep_south
-                later[i] = value
-            now = later
-        for r in range(rows):
-            smooth[pl.ds(r * smooth_step + first, 8), :] = now[HALO + r] * (mixing_rate**DIFF_STEPS)
-
-    by_levels(diffuse)
+            state = [sweep_rows(now, sweep) for now in state]
+        for first, now in zip(firsts, state):
+            for r in range(rows):
+                smooth[pl.ds(r * smooth_step + first, 8), :] = now[HALO + r] * (mixing_rate**DIFF_STEPS)
+        return 0
+
+    lax.fori_loop(0, (len(blocks) + TOGETHER - 1) // TOGETHER, diffuse, 0)
+    smooth_copy = pltpu.make_async_copy(smooth, smooth_hbm, out_sem.at[1])
+    smooth_copy.start()
 
     mats_copy.wait()
     for copy in to_side:
@@ -394,6 +398,8 @@
         term = jnp.dot(part, mats[...], preferred_element_type=F32)
         total = term if total is None else total + term
     fix[...] = total * (mixing_rate**DIFF_STEPS)
+    fix_copy = pltpu.make_async_copy(fix, fix_hbm, out_sem.at[2])
+    fix_copy.start()
 
     @pl.when(has_north)
     def _():
@@ -407,14 +413,26 @@
 
     for copy in to_side:
         copy.wait_send()
-
-
-def finish(rows, levels, heat, smooth, fix, heat_hbm, smooth_hbm, fixed, ordered, sem):
+    for copy in (heat_copy, smooth_copy, fix_copy):
+        copy.wait()
+
+
+def finish(
+    rows, levels, heat, smooth_in, fix_in, heat_hbm, smooth_hbm, smooth, fix, fixed, ordered, in_sem, sem
+):
     lanes = heat.shape[1]
     half = rows // 2
     step = smooth.shape[0] // rows
+    loads = [
+        pltpu.make_async_copy(smooth_in, smooth, in_sem.at[0]),
+        pltpu.make_async_copy(fix_in, fix, in_sem.at[1]),
+    ]
+    for copy in loads:
+        copy.start()
     heat_copy = pltpu.make_async_copy(heat, heat_hbm, sem.at[0])
     heat_copy.start()
+    for copy in loads:
+        copy.wait()
     lane_row = lax.broadcasted_iota(jnp.int32, (8, lanes), 1) // EDGE
     copies, done = [heat_copy], 0
     for first in [*range(0, levels - 7, 8)] + ([levels - 8] if levels % 8 else []):
@@ -448,7 +466,7 @@
         return jnp.swapaxes(x, 0, 1).reshape(levels * rows, lanes)
 
     shape = jax.ShapeDtypeStruct((levels * rows, lanes), F32)
-    vmem, smem, hbm = (pl.BlockSpec(memory_space=m) for m in (pltpu.VMEM, pltpu.SMEM, pltpu.HBM))
+    hbm = pl.BlockSpec(memory_space=pltpu.HBM)
     n_copies = 2 + 3 * n_sides
     deep = (levels + 7) // 8 * 8
     heat, smooth, fix = pl.pallas_call(
@@ -458,30 +476,37 @@
             jax.ShapeDtypeStruct((rows * (slab - 1), lanes), F32),
             jax.ShapeDtypeStruct((deep, lanes), F32),
         ),
-        in_specs=[hbm, hbm, hbm, hbm, vmem, smem, smem],
-        out_specs=(vmem, vmem, vmem),
+        in_specs=[hbm] * 7,
+        out_specs=(hbm, hbm, hbm),
         scratch_shapes=[
             pltpu.VMEM((rows * levels * points, lanes), jnp.bfloat16),
             pltpu.VMEM((levels * rows, lanes), jnp.bfloat16),
             pltpu.VMEM((levels * rows, lanes), F32),
             pltpu.VMEM(mats.shape[1:], jnp.bfloat16),
+            pltpu.VMEM((rows, lanes), jnp.bfloat16),
+            pltpu.SMEM((1, rows), jnp.int32),
+            pltpu.SMEM((points,), F32),
             pltpu.VMEM((8 * (levels * points + 1), lanes), F32),
             pltpu.VMEM((levels, points, 8, lanes), F32),
             pltpu.VMEM((levels, points, 8, lanes), F32),
             pltpu.VMEM((levels, 8, lanes), F32),
             pltpu.VMEM((levels, 8, lanes), F32),
+            pltpu.VMEM((levels * rows, lanes), F32),
+            pltpu.VMEM((rows * (slab - 1), lanes), F32),
+            pltpu.VMEM((deep, lanes), F32),
             pltpu.VMEM(((rows + 2 * HALO) * slab, lanes), F32),
             pltpu.VMEM((levels, lanes), F32),
             pltpu.VMEM((2, deep // 32, 8, lanes), F32),
             pltpu.VMEM((n_sides, levels, lanes), F32),
             pltpu.VMEM((2, n_sides, deep // 32, 8, lanes), F32),
             pltpu.VMEM((deep, 2 * lanes), F32),
-            pltpu.SemaphoreType.DMA((8,)),
+            pltpu.SemaphoreType.DMA((12,)),
+            pltpu.SemaphoreType.DMA((3,)),
             pltpu.SemaphoreType.DMA((n_copies,)),
             pltpu.SemaphoreType.DMA((n_copies,)),
         ],
         compiler_params=pltpu.CompilerParams(
-            collective_id=0, has_side_effects=True, vmem_limit_bytes=20 * 1024 * 1024
+            collective_id=0, has_side_effects=True, vmem_limit_bytes=56 * 1024 * 1024
         ),
     )(
         optical_depth.reshape(rows * levels * points, lanes),
@@ -490,14 +515,17 @@
     heating, smoothed = pl.pallas_call(
         functools.partial(finish, rows, levels),
         out_shape=(shape, shape),
-        in_specs=[vmem, vmem, vmem],
+        in_specs=[hbm] * 3,
         out_specs=(hbm, hbm),
         scratch_shapes=[
             pltpu.VMEM((rows * (slab - 1), lanes), F32),
+            pltpu.VMEM((deep, lanes), F32),
+            pltpu.VMEM((rows * (slab - 1), lanes), F32),
             pltpu.VMEM((levels * rows, lanes), F32),
+            pltpu.SemaphoreType.DMA((2,)),
             pltpu.SemaphoreType.DMA((2 + levels // CHUNK + 1,)),
         ],
-        compiler_params=pltpu.CompilerParams(vmem_limit_bytes=20 * 1024 * 1024),
+        compiler_params=pltpu.CompilerParams(vmem_limit_bytes=56 * 1024 * 1024),
     )(heat, smooth, fix)
     return tuple(jnp.swapaxes(x.reshape(levels, rows, lanes), 0, 1) for x in (heating, smoothed))
 

time: 23.7 us -> 38.1 us (1.61)
  Pallas kernels: 16.4 us -> 37.3 us
  local copies, waits for them, and re-layouts: 6.41 us -> 0 us
    pallas_call x1, Pallas kernels: 1.15 us -> 23.5 us  [per_device(): pl.pallas_call(functools.partial(finish, rows, levels), out_shape=(shape,...]
    unnamed x14 -> x0, local copies, waits for them, and re-layouts: 6.41 us -> none
    pallas_call x1, Pallas kernels: 15.2 us -> 13.8 us  [per_device(): pl.pallas_call(functools.partial(kernel, n_tiles, n_band, rows, levels, p...]
where the time goes in v4:
time: 38.1 us; the launch traced here: 38 us
  Pallas kernels  37.3 us (98%)
  between operations  0.64 us (2%)
    pallas_call x1, Pallas kernels, per_device(): pl.pallas_call(functools.partial(finish, rows, levels), out_shape=(shape,...  23.5 us
    pallas_call x1, Pallas kernels, per_device(): pl.pallas_call(functools.partial(kernel, n_tiles, n_band, rows, levels, p...  13.8 us

profile of v4, /device:TPU:9, one launch (start us, length us, event | category | flops | bytes accessed | tf_op | source)
XLA Modules:
  0.0 38.0 jit_solution(14046291532201279200)
XLA Ops:
  0.6 13.8 %shard_map.86 = (f32[1440,128]{1,0:T(8,128)}, f32[1552,128]{1,0:T(8,128)}, f32[96,128]{1,0:T(8,128)}) custom-call(bf16[5760,128]{1,0:T(8,128)(2,1)} %bitcast.14, bf16[1440,128]{1,0:T(8,128)(2,1)} %bitcast.16, f32[1440,128]{1,0:T(8,128)} %bitcast.15, bf16[4,256,128]{2,1,0:T(8,128)(2,1)} %constant.2.clone.mats_hbm, bf16[16,128]{1,0:T(8,128)(2,1)} %insolation_hbm.1, ...), custom_call_target="tpu_custom_call" | custom-call | tf_op jit(solution)/shard_map/pallas_call | solution.py:472
  14.4 23.5 %shard_map.87 = (f32[1440,128]{1,0:T(8,128)}, f32[1440,128]{1,0:T(8,128)}) custom-call(f32[1440,128]{1,0:T(8,128)} %get-tuple-element.7.heat, f32[1552,128]{1,0:T(8,128)} %get-tuple-element.8.smooth_in, f32[96,128]{1,0:T(8,128)} %get-tuple-element.9.fix_in), custom_call_target="tpu_custom_call" | custom-call | tf_op jit(solution)/shard_map/pallas_call | solution.py:515
